TPU v7x, 32 devices: a whole 2x2x4 slice. The times are simulated.
32 devices in a mesh: clip: 4 (over y, x), seq: 8 (over z, core).
Axes of the slice: x: 2, y: 2, z: 4, core: 2. Of those that a mesh axis runs over, the one named last changes fastest.
Arguments:
- frames_in: bfloat16 [128, 64, 1152], P(('clip', 'seq')), parts along dimension 0, may hold values from -6 to 6
- modulation: float32 [12, 1152], P('clip'), parts along dimension 0, may hold values from -3 to 3
- self_proj: bfloat16 [1152, 1728], P(None, 'seq'), may hold values from -0.1875 to 0.1875
- self_out: bfloat16 [576, 1152], P(None, 'seq'), may hold values from -0.25 to 0.25
- cross_query: bfloat16 [1152, 576], P(None, 'seq'), may hold values from -0.1875 to 0.1875
- cross_keyval: bfloat16 [1152, 1152], P(None, 'seq'), may hold values from -0.1875 to 0.1875
- cross_out: bfloat16 [576, 1152], P(None, 'seq'), may hold values from -0.25 to 0.25
- text_bank: bfloat16 [8, 256, 1152], P('seq'), may hold values from -6 to 6
- prompt_pick: int32 [4], P('clip'), parts along dimension 0, may hold values from 0 to 7
- text_lengths: int32 [8], replicated, may hold values from 32 to 256
Outputs:
- frames_out: bfloat16 [128, 64, 1152], P(('clip', 'seq')), parts along dimension 0
There are 4 independent parts, one for each index of `clip`. A program takes and returns all parts, laid end to end along the dimension named above; an argument that names none is the same for every part. Nothing has to cross between parts.
All inputs are finite; a program needn't handle non-finite values.
Results may differ from a plain program's by a relative error of at most 0.006.
Values may be sent and summed in bfloat16 or wider, within the bound.
A program may use at most 64 MiB of HBM per device.

v0:
```python
import math

import jax
import jax.numpy as jnp
from jax import lax
from jax.sharding import PartitionSpec as P

HEAD_DIM = 72


EPS = 1e-06


def spread_2(block, axis, owner):
    block = jnp.where(lax.axis_index(axis) == owner, block, jnp.zeros_like(block))
    return lax.psum(block, axis)


def layer_norm(values):
    mean = jnp.mean(values, axis=-1, keepdims=True)
    centred = values - mean
    spread = jnp.mean(centred * centred, axis=-1, keepdims=True)
    return centred * lax.rsqrt(spread + EPS)


def head_norm(values, heads):
    shaped = values.reshape(values.shape[:-1] + (heads, values.shape[-1] // heads))
    power = jnp.mean(shaped * shaped, axis=-1, keepdims=True)
    return shaped * lax.rsqrt(power + EPS)


def temporal_attention(qkv, heads, attn, scale_q):
    frames, patches = (qkv.shape[0], qkv.shape[1])
    query = (head_norm(qkv[..., :attn].astype(jnp.float32), heads) * scale_q).astype(jnp.bfloat16)
    key = head_norm(qkv[..., attn : 2 * attn].astype(jnp.float32), heads).astype(jnp.bfloat16)
    value = qkv[..., 2 * attn :].reshape(frames, patches, heads, attn // heads)
    scores = jnp.einsum("fphd,gphd->phfg", query, key, preferred_element_type=jnp.float32)
    weights = jnp.exp(scores)
    total = jnp.sum(weights, axis=-1)
    probs = weights.astype(jnp.bfloat16)
    mixed = jnp.einsum("phfg,gphd->fphd", probs, value, preferred_element_type=jnp.float32)
    attended = mixed / jnp.transpose(total, (2, 0, 1))[..., None]
    return attended.astype(jnp.bfloat16).reshape(frames, patches, attn)


def per_device(
    frames_in,
    modulation,
    self_proj,
    self_out,
    cross_query,
    cross_keyval,
    cross_out,
    text_bank,
    prompt_pick,
    text_lengths,
):
    count = lax.axis_size("seq")
    frame_rows, pixels, width = frames_in.shape
    attn = self_out.shape[0]
    heads = attn // HEAD_DIM
    scale_q = 1.0 / math.sqrt(HEAD_DIM)
    pix_dev = pixels // count
    frames = frame_rows * count
    tokens = frames_in.astype(jnp.float32)
    normed = (layer_norm(tokens) * (1.0 + modulation[1]) + modulation[0]).astype(jnp.bfloat16)
    switched = lax.all_to_all(normed, "seq", split_axis=1, concat_axis=0, tiled=True)
    flat_pix = switched.reshape(-1, width)
    qkv = jnp.dot(
        flat_pix,
        lax.all_gather(self_proj, "seq", axis=1, tiled=True),
        preferred_element_type=jnp.float32,
    ).astype(jnp.bfloat16)
    qkv = qkv.reshape(frames, pix_dev, 3 * attn)
    out_self, query_weight, out_cross = (
        lax.all_gather(self_out, "seq", axis=1, tiled=True),
        lax.all_gather(cross_query, "seq", axis=1, tiled=True),
        lax.all_gather(cross_out, "seq", axis=1, tiled=True),
    )
    attended = temporal_attention(qkv, heads, attn, scale_q)
    returned = lax.all_to_all(attended, "seq", split_axis=0, concat_axis=1, tiled=True)
    self_term = jnp.dot(returned.reshape(-1, attn), out_self, preferred_element_type=jnp.float32)
    after_self = (tokens.reshape(-1, width) + modulation[2] * self_term).astype(jnp.bfloat16)
    pick = prompt_pick[0]
    memory = spread_2(text_bank[0], "seq", pick)
    own_columns = jnp.dot(memory, cross_keyval, preferred_element_type=jnp.float32).astype(
        jnp.bfloat16
    )
    keyval = lax.all_gather(own_columns, "seq", axis=1, tiled=True)
    text_len = keyval.shape[0]
    text_key = head_norm(keyval[:, :attn].astype(jnp.float32), heads).astype(jnp.bfloat16)
    text_value = keyval[:, attn:].reshape(text_len, heads, HEAD_DIM)
    slots = jnp.arange(text_lengths.shape[0], dtype=jnp.int32)
    length = jnp.sum(jnp.where(slots == pick, text_lengths, 0))
    live = jnp.arange(text_len, dtype=jnp.int32) < length
    text_query = jnp.dot(after_self, query_weight, preferred_element_type=jnp.float32)
    text_query = (head_norm(text_query, heads) * scale_q).astype(jnp.bfloat16)
    cross_scores = jnp.einsum(
        "thd,lhd->thl", text_query, text_key, preferred_element_type=jnp.float32
    )
    cross_weights = jnp.where(live, jnp.exp(cross_scores), 0.0)
    cross_total = jnp.sum(cross_weights, axis=-1)
    cross_probs = cross_weights.astype(jnp.bfloat16)
    cross_mix = jnp.einsum(
        "thl,lhd->thd", cross_probs, text_value, preferred_element_type=jnp.float32
    )
    crossed = (cross_mix / cross_total[..., None]).astype(jnp.bfloat16).reshape(-1, attn)
    cross_term = jnp.dot(crossed, out_cross, preferred_element_type=jnp.float32)
    frames_out = (after_self.astype(jnp.float32) + cross_term).astype(jnp.bfloat16)
    return frames_out.reshape(frame_rows, pixels, width)


def solution(mesh):
    placed = (
        P(("clip", "seq"), None, None),
        P("clip", None),
        P(None, "seq"),
        P(None, "seq"),
        P(None, "seq"),
        P(None, "seq"),
        P(None, "seq"),
        P("seq", None, None),
        P("clip"),
        P(),
    )
    return jax.shard_map(
        per_device,
        mesh=mesh,
        in_specs=placed,
        out_specs=P(("clip", "seq"), None, None),
        check_vma=False,
    )
```

profile of v0, /device:TPU:1, one launch (start us, length us, event | category | flops | bytes accessed | tf_op | source)
XLA Modules:
  0.0 213.4 jit_solution(6026191553684569355)
XLA Ops:
  7.3 0.9 select_bitcast_fusion
  8.1 0.0 all-reduce.2.cloned.1.call-update
  8.2 0.0 all-gather.5.cloned.1.call-start
  8.2 0.7 all-gather.5.cloned.1.call-update
  8.9 0.0 all-gather.7.cloned.1.call-start
  9.0 0.7 all-gather.7.cloned.1.call-update
  9.7 0.0 all-gather.9.cloned.1.call-start
  9.7 0.5 all-gather.9.cloned.1.call-update
  10.3 0.5 convert_reduce_fusion
  10.8 0.6 multiply_reduce_fusion
  11.4 1.5 add_convert_fusion
  12.9 6.5 %all-to-all-start = ((bf16[4,64,1152]{2,0,1:T(4,128)(2,1)}), bf16[4,64,1152]{2,0,1:T(4,128)(2,1)S(1)}, u32[]{:S(2)}, u32[]{:S(2)}) async-start(bf16[4,64,1152]{2,0,1:T(4,128)(2,1)} %add_convert_fusion), calls=%async_computation | async-start | bytes 1179648 | tf_op jit(solution)/shard_map/all_to_all | solution.py:67
  19.4 0.6 all-gather.11.cloned.1.call-update
  20.0 0.5 copy_convert_fusion
  20.5 0.0 copy-start.5
  20.5 1.2 copy.31
  21.7 0.6 fusion.20
  22.3 0.6 iota_compare_fusion
  22.9 49.6 %all-reduce.2.cloned.1.call-done = bf16[256,1152]{1,0:T(8,128)(2,1)} async-done(((bf16[256,1152]{1,0:T(8,128)(2,1)}), bf16[256,1152]{1,0:T(8,128)(2,1)}) %all-reduce.2.cloned.1.call-update) | async-done | bytes 589840 | tf_op jit(solution)/shard_map/psum | solution.py:16
  72.5 1.4 convolution_convert_fusion.1
  73.9 20.5 %all_gather.17 = bf16[256,1152]{0,1:T(8,128)(2,1)} all-gather(bf16[256,144]{0,1:T(8,128)(2,1)S(1)} %convolution_convert_fusion.1), channel_id=1, replica_groups=mesh['clip'=4,'seq'=8] {'seq'}, dimensions={1}, use_global_device_ids=true | all-gather | bytes 663552 | tf_op jit(solution)/shard_map/all_gather | solution.py:89
  94.4 0.1 copy.59
  94.5 26.9 %all-gather.5.cloned.1.call-done = bf16[1152,1728]{0,1:T(8,128)(2,1)} async-done(((bf16[1152,216]{0,1:T(8,128)(2,1)}), bf16[1152,1728]{0,1:T(8,128)(2,1)}) %all-gather.5.cloned.1.call-update) | async-done | bytes 3981328 | tf_op jit(solution)/shard_map/all_gather | solution.py:71
  121.4 3.5 %convolution_convert_fusion = bf16[256,1728]{0,1:T(8,128)(2,1)S(1)} fusion(bf16[256,1152]{1,0:T(8,128)(2,1)S(1)} %bitcast.63, bf16[1152,1728]{0,1:T(8,128)(2,1)} %all-gather.5.cloned.1.call-done), kind=kOutput, calls=%fused_computation.4 | convolution fusion | flops 1019658240 | bytes 5455872 | tf_op jit(solution)/shard_map/dot_general | solution.py:69
  124.9 0.6 copy.34
  125.5 0.2 slice_convert_fusion.1
  125.7 0.5 reshape.126
  126.2 0.3 multiply_reduce_fusion.1
  126.6 0.5 reshape.124
  127.1 0.3 multiply_reduce_fusion.2
  127.5 0.6 reshape.110
  128.0 0.7 multiply_convert_fusion
  128.7 0.9 fusion.24
  129.7 0.7 fusion.4
  130.4 0.2 copy.39
  130.6 1.1 reshape.115
  131.7 3.7 %all-to-all-start.1 = ((bf16[32,8,576]{2,1,0:T(8,128)(2,1)}), bf16[32,8,576]{2,1,0:T(8,128)(2,1)S(1)}, u32[]{:S(2)}, u32[]{:S(2)}) async-start(bf16[32,8,576]{2,1,0:T(8,128)(2,1)} %reshape.115), calls=%async_computation.1 | async-start | bytes 655360 | tf_op jit(solution)/shard_map/all_to_all | solution.py:81
  135.5 0.1 fusion.9
  135.6 17.5 %all-to-all-done.1 = bf16[32,8,576]{2,1,0:T(8,128)(2,1)S(1)} async-done(((bf16[32,8,576]{2,1,0:T(8,128)(2,1)}), bf16[32,8,576]{2,1,0:T(8,128)(2,1)S(1)}, u32[]{:S(2)}, u32[]{:S(2)}) %all-to-all-start.1) | async-done | bytes 294944 | tf_op jit(solution)/shard_map/all_to_all | solution.py:81
  153.1 1.5 all-gather.7.cloned.1.call-done
  154.6 2.1 fusion.2
  156.6 21.8 %all-gather.9.cloned.1.call-done = bf16[1152,576]{0,1:T(8,128)(2,1)} async-done(((bf16[1152,72]{0,1:T(8,128)(2,1)}), bf16[1152,576]{0,1:T(8,128)(2,1)}) %all-gather.9.cloned.1.call-update) | async-done | bytes 1327120 | tf_op jit(solution)/shard_map/all_gather | solution.py:77
  178.5 1.9 fusion.25
  180.4 0.1 multiply_reduce_fusion.3
  180.5 0.6 bitcast_reduce_fusion
  181.0 0.5 fusion.6
  181.5 22.4 %all-gather.11.cloned.1.call-done = bf16[576,1152]{0,1:T(8,128)(2,1)} async-done(((bf16[576,144]{0,1:T(8,128)(2,1)}), bf16[576,1152]{0,1:T(8,128)(2,1)}) %all-gather.11.cloned.1.call-update) | async-done | bytes 1327120 | tf_op jit(solution)/shard_map/all_gather | solution.py:78
  203.9 2.9 %fusion.1 = bf16[256,1152]{1,0:T(8,128)(2,1)} fusion(bf16[256,576]{0,1:T(8,128)(2,1)S(1)} %bitcast.64, bf16[576,1152]{0,1:T(8,128)(2,1)} %all-gather.11.cloned.1.call-done, bf16[256,1152]{1,0:T(8,128)(2,1)S(1)} %fusion.2), kind=kOutput, calls=%fused_computation.3 | convolution fusion | flops 340623360 | bytes 2801664 | tf_op jit(solution)/shard_map/dot_general | solution.py:108
  (24 shorter events, 0.3 us)
Async XLA Ops:
  6.5 66.0 %copy-start = (bf16[1152,144]{0,1:T(8,128)(2,1)S(1)}, bf16[1152,144]{0,1:T(8,128)(2,1)}, u32[]{:S(2)}) copy-start(bf16[1152,144]{0,1:T(8,128)(2,1)} %param.15) | copy-start | bytes 995332
  6.5 3.7 %copy-start.4 = (f32[3,1152]{1,0:T(4,128)S(1)}, f32[3,1152]{1,0:T(4,128)}, u32[]{:S(2)}) copy-start(f32[3,1152]{1,0:T(4,128)} %param.11) | copy-start | bytes 41476
  6.5 66.0 %all-reduce.2.cloned.1.call-start = ((), (), s32[]{:S(2)}) async-start(), calls=%async_computation.4 | async-start | bytes 1179648 | tf_op jit(solution)/shard_map/psum | solution.py:16
  7.3 3.0 %copy-start.1 = (bf16[4,64,1152]{2,1,0:T(8,128)(2,1)S(1)}, bf16[4,64,1152]{2,1,0:T(8,128)(2,1)}, u32[]{:S(2)}) copy-start(bf16[4,64,1152]{2,1,0:T(8,128)(2,1)} %param.10) | copy-start | bytes 1769476
  8.2 113.2 %all-gather.5.cloned.1.call-start = ((), (), s32[]{:S(2)}) async-start(), calls=%async_computation.2 | async-start | bytes 4478976 | tf_op jit(solution)/shard_map/all_gather | solution.py:71
  8.9 145.6 %all-gather.7.cloned.1.call-start = ((), (), s32[]{:S(2)}) async-start(), calls=%async_computation.3 | async-start | bytes 1658880 | tf_op jit(solution)/shard_map/all_gather | solution.py:76
  9.7 168.8 %all-gather.9.cloned.1.call-start = ((), (), s32[]{:S(2)}) async-start(), calls=%async_computation.5 | async-start | bytes 1492992 | tf_op jit(solution)/shard_map/all_gather | solution.py:77
  12.9 81.5 %all-to-all-start = ((bf16[4,64,1152]{2,0,1:T(4,128)(2,1)}), bf16[4,64,1152]{2,0,1:T(4,128)(2,1)S(1)}, u32[]{:S(2)}, u32[]{:S(2)}) async-start(bf16[4,64,1152]{2,0,1:T(4,128)(2,1)} %add_convert_fusion), calls=%async_computation | async-start | bytes 1179648 | tf_op jit(solution)/shard_map/all_to_all | solution.py:67
  19.4 184.5 %all-gather.11.cloned.1.call-start = ((), (), s32[]{:S(2)}) async-start(), calls=%async_computation.6 | async-start | bytes 1658880 | tf_op jit(solution)/shard_map/all_gather | solution.py:78
  20.5 1.2 copy-start.5
  130.4 5.1 %copy-start.3 = (bf16[256,1152]{0,1:T(8,128)(2,1)S(1)}, bf16[256,1152]{0,1:T(8,128)(2,1)}, u32[]{:S(2)}) copy-start(bf16[256,1152]{0,1:T(8,128)(2,1)} %all_gather.17) | copy-start | bytes 1769476
  131.7 22.9 %copy-start.2 = (f32[4,64,1152]{2,1,0:T(8,128)S(1)}, f32[4,64,1152]{2,1,0:T(8,128)}, u32[]{:S(2)}) copy-start(f32[4,64,1152]{2,1,0:T(8,128)} %copy.31) | copy-start | bytes 3538948
  131.7 21.4 %all-to-all-start.1 = ((bf16[32,8,576]{2,1,0:T(8,128)(2,1)}), bf16[32,8,576]{2,1,0:T(8,128)(2,1)S(1)}, u32[]{:S(2)}, u32[]{:S(2)}) async-start(bf16[32,8,576]{2,1,0:T(8,128)(2,1)} %reshape.115), calls=%async_computation.1 | async-start | bytes 655360 | tf_op jit(solution)/shard_map/all_to_all | solution.py:81
Sparse Core Ops, SparseCore 0:
  9.7 62.7 all-reduce.1
  74.2 47.2 all-gather.4
  123.1 31.4 all-gather.6
  156.0 22.3 all-gather.8
  180.0 23.9 all-gather.10
where the time goes:
time: 214 us; the launch traced here: 213 us
  waiting for transfers between devices  142 us (66%)
  blocking collectives  20.5 us (10%)
  matrix products  14.4 us (7%)
  between operations  14.1 us (7%)
  starting transfers between devices  10.4 us (5%)
  other arithmetic  7.05 us (3%)
  local copies, waits for them, and re-layouts  4.81 us (2%)
    psum x1, waiting for transfers between devices, spread_2(): return lax.psum(block, axis)  49.6 us
    all_gather x1, waiting for transfers between devices, per_device(): lax.all_gather(self_proj, 'seq', axis=1, tiled=True)  26.9 us
    all_gather x1, waiting for transfers between devices, per_device(): lax.all_gather(cross_out, 'seq', axis=1, tiled=True)  22.4 us
    all_gather x1, waiting for transfers between devices, per_device(): lax.all_gather(cross_query, 'seq', axis=1, tiled=True)  21.8 us
    all_gather x1, blocking collectives, per_device(): keyval = lax.all_gather(own_columns, 'seq', axis=1, tiled=True)  20.5 us
    all_to_all x1, waiting for transfers between devices, per_device(): lax.all_to_all(attended, 'seq', split_axis=0, concat_axis=1, tiled=True)  17.5 us
    all_to_all x1, starting transfers between devices, per_device(): lax.all_to_all(normed, 'seq', split_axis=1, concat_axis=0, tiled=True)  6.49 us
  transfers between devices with their start and end apart: 7, of which 6 were waited for; matrix products, arithmetic and copies ran while one was open for 11% of the time, Pallas kernels for 0%

commit v1 on v0

--- a/solution.py
+++ b/solution.py
@@ -1,8 +1,11 @@
+import functools
 import math
 
 import jax
 import jax.numpy as jnp
 from jax import lax
+from jax.experimental import pallas as pl
+from jax.experimental.pallas import tpu as pltpu
 from jax.sharding import PartitionSpec as P
 
 HEAD_DIM = 72
@@ -110,7 +113,307 @@
     return frames_out.reshape(frame_rows, pixels, width)
 
 
+MESH = pl.DeviceIdType.MESH
+CLIPS, LEVELS, CORES = 4, 4, 2
+
+
+def greet(peers):
+    barrier = pltpu.get_barrier_semaphore()
+    for peer in peers:
+        pl.semaphore_signal(barrier, inc=1, device_id=peer, device_id_type=MESH)
+    pl.semaphore_wait(barrier, len(peers))
+
+
+def places():
+    clip, seq = lax.axis_index("clip"), lax.axis_index("seq")
+    level, core = seq // CORES, seq % CORES
+    sibling = level * CORES + (1 - core)
+    levels = [lax.rem(level + step, LEVELS) for step in range(1, LEVELS)]
+    clips = [lax.rem(clip + step, CLIPS) for step in range(1, CLIPS)]
+    return clip, seq, level, core, sibling, levels, clips
+
+
+def remote(src, dst, send_sem, recv_sem, clip, seq):
+    return pltpu.make_async_remote_copy(
+        src_ref=src,
+        dst_ref=dst,
+        send_sem=send_sem,
+        recv_sem=recv_sem,
+        device_id=(clip, seq),
+        device_id_type=MESH,
+    )
+
+
+def gather_kernel(
+    blocks_ref, pack_ref, memory_ref, tokens_ref, weights_ref, rows_ref,
+    half_ref, slots_ref, held_ref,
+    block_send, block_recv, pack_send, pack_recv, local_sem, half_sem, slice_send, slice_recv,
+):
+    clip, seq, level, core, sibling, levels, clips = places()
+    peers = [lax.rem(seq + step, LEVELS * CORES) for step in range(1, LEVELS * CORES)]
+    greet([(clip, peer) for peer in peers] + [(other, seq) for other in clips])
+    piece = pack_ref.shape[0] // CLIPS
+    pieces = [clip] + clips
+
+    def rows(index):
+        return pl.ds(pl.multiple_of(index * piece, 16), piece)
+
+    own_rows = [pltpu.make_async_copy(pack_ref, weights_ref.at[seq], local_sem.at[0]),
+                pltpu.make_async_copy(blocks_ref.at[seq], tokens_ref.at[seq], local_sem.at[1])]
+    for copy in own_rows:
+        copy.start()
+    half = held_ref.shape[0]
+    swap = remote(
+        memory_ref.at[pl.ds(pl.multiple_of((1 - core) * half, 16), half)], half_ref,
+        half_sem.at[0], half_sem.at[1], clip, sibling,
+    )
+    swap.start()
+    sends = [swap]
+
+    def weight(src, shard, part, index, to_clip, to_seq):
+        copy = remote(
+            src, weights_ref.at[shard, rows(part)], pack_send.at[index],
+            pack_recv.at[shard, part], to_clip, to_seq,
+        )
+        copy.start()
+        sends.append(copy)
+
+    def arrived(shard, part):
+        view = weights_ref.at[shard, rows(part)]
+        pltpu.make_async_copy(view, view, pack_recv.at[shard, part]).wait()
+
+    for n, other in enumerate(levels):
+        weight(pack_ref.at[rows(clip)], seq, clip, n, clip, other * CORES + core)
+    for n, peer in enumerate(peers):
+        copy = remote(
+            blocks_ref.at[peer], tokens_ref.at[seq], block_send.at[n], block_recv.at[seq], clip, peer
+        )
+        copy.start()
+        sends.append(copy)
+    for n, part in enumerate(pieces):
+        weight(pack_ref.at[rows(part)], seq, part, 3 + n, clip, sibling)
+
+    swap.wait_recv()
+    held_ref[...] = memory_ref[pl.ds(pl.multiple_of(core * half, 16), half)] + half_ref[...]
+    size = half // LEVELS
+    slices = []
+    for n, other in enumerate(levels):
+        copy = remote(
+            held_ref.at[pl.ds(pl.multiple_of(other * size, 16), size)], slots_ref.at[level],
+            slice_send.at[n], slice_recv.at[level], clip, other * CORES + core,
+        )
+        copy.start()
+        sends.append(copy)
+
+    index = 7
+    for other in levels:
+        shard = other * CORES + core
+        arrived(shard, clip)
+        for to in clips:
+            weight(weights_ref.at[shard, rows(clip)], shard, clip, index, to, seq)
+            index += 1
+        weight(weights_ref.at[shard, rows(clip)], shard, clip, index, clip, sibling)
+        index += 1
+    for other in levels:
+        shard = other * CORES + core
+        for part in clips:
+            arrived(shard, part)
+            weight(weights_ref.at[shard, rows(part)], shard, part, index, clip, sibling)
+            index += 1
+
+    total = held_ref[pl.ds(pl.multiple_of(level * size, 16), size)]
+    for other in levels:
+        pltpu.make_async_copy(slots_ref.at[other], slots_ref.at[other], slice_recv.at[other]).wait()
+        total = total + slots_ref[other]
+    rows_ref[...] = total
+    for other in [level] + levels:
+        for part in pieces:
+            arrived(other * CORES + 1 - core, part)
+    for peer in peers:
+        view = tokens_ref.at[peer]
+        pltpu.make_async_copy(view, view, block_recv.at[peer]).wait()
+    for copy in own_rows:
+        copy.wait()
+    for copy in sends:
+        copy.wait_send()
+
+
+def gather(blocks, pack, memory):
+    count, rows, width = blocks.shape
+    text, dma = memory.shape[0], pltpu.SemaphoreType.DMA
+    anywhere = pl.BlockSpec(memory_space=pl.ANY)
+    vmem = pl.BlockSpec(memory_space=pltpu.VMEM)
+    size = text // count
+    return pl.pallas_call(
+        gather_kernel,
+        out_shape=(
+            jax.ShapeDtypeStruct(blocks.shape, blocks.dtype),
+            jax.ShapeDtypeStruct((count,) + pack.shape, pack.dtype),
+            jax.ShapeDtypeStruct((size, width), memory.dtype),
+        ),
+        in_specs=[anywhere, anywhere, vmem],
+        out_specs=(anywhere, anywhere, vmem),
+        scratch_shapes=[
+            pltpu.VMEM((text // CORES, width), memory.dtype),
+            pltpu.VMEM((LEVELS, size, width), memory.dtype),
+            pltpu.VMEM((text // CORES, width), memory.dtype),
+            dma((count - 1,)),
+            dma((count,)),
+            dma((28,)),
+            dma((count, CLIPS)),
+            dma((2,)),
+            dma((2,)),
+            dma((LEVELS - 1,)),
+            dma((LEVELS,)),
+        ],
+        compiler_params=pltpu.CompilerParams(collective_id=0, has_side_effects=True),
+    )(blocks, pack, memory)
+
+
+def return_kernel(blocks_ref, text_ref, tokens_ref, keyval_ref,
+                  block_send, block_recv, text_send, text_recv, local_sem):
+    clip, seq, level, core, sibling, levels, _ = places()
+    peers = [lax.rem(seq + step, LEVELS * CORES) for step in range(1, LEVELS * CORES)]
+    greet([(clip, peer) for peer in peers])
+    own = [pltpu.make_async_copy(text_ref, keyval_ref.at[seq], local_sem.at[0]),
+           pltpu.make_async_copy(blocks_ref.at[seq], tokens_ref.at[seq], local_sem.at[1])]
+    for copy in own:
+        copy.start()
+    sends = []
+
+    def text(src, shard, index, to):
+        copy = remote(src, keyval_ref.at[shard], text_send.at[index], text_recv.at[shard], clip, to)
+        copy.start()
+        sends.append(copy)
+
+    def arrived(ref, sem, shard):
+        pltpu.make_async_copy(ref.at[shard], ref.at[shard], sem.at[shard]).wait()
+
+    for n, other in enumerate(levels):
+        text(text_ref, seq, n, other * CORES + core)
+    for n, peer in enumerate(peers):
+        copy = remote(
+            blocks_ref.at[peer], tokens_ref.at[seq], block_send.at[n], block_recv.at[seq], clip, peer
+        )
+        copy.start()
+        sends.append(copy)
+    text(text_ref, seq, 3, sibling)
+    for n, other in enumerate(levels):
+        shard = other * CORES + core
+        arrived(keyval_ref, text_recv, shard)
+        text(keyval_ref.at[shard], shard, 4 + n, sibling)
+    for other in [level] + levels:
+        arrived(keyval_ref, text_recv, other * CORES + 1 - core)
+    for peer in peers:
+        arrived(tokens_ref, block_recv, peer)
+    for copy in own:
+        copy.wait()
+    for copy in sends:
+        copy.wait_send()
+
+
+def give_back(blocks, text):
+    count, dma = blocks.shape[0], pltpu.SemaphoreType.DMA
+    anywhere = pl.BlockSpec(memory_space=pl.ANY)
+    return pl.pallas_call(
+        return_kernel,
+        out_shape=(
+            jax.ShapeDtypeStruct(blocks.shape, blocks.dtype),
+            jax.ShapeDtypeStruct((count,) + text.shape, text.dtype),
+        ),
+        in_specs=[anywhere, anywhere],
+        out_specs=(anywhere, anywhere),
+        scratch_shapes=[dma((count - 1,)), dma((count,)), dma((7,)), dma((count,)), dma((2,))],
+        compiler_params=pltpu.CompilerParams(collective_id=1, has_side_effects=True),
+    )(blocks, text)
+
+
+def nt(left, right):
+    return lax.dot_general(
+        left, right, (((1,), (1,)), ((), ())), preferred_element_type=jnp.float32
+    )
+
+
+def per_device_shared(
+    frames_in,
+    modulation,
+    self_proj,
+    self_out,
+    cross_query,
+    cross_keyval,
+    cross_out,
+    text_bank,
+    prompt_pick,
+    text_lengths,
+):
+    count = lax.axis_size("seq")
+    frame_rows, pixels, width = frames_in.shape
+    attn = self_out.shape[0]
+    heads = attn // HEAD_DIM
+    scale_q = 1.0 / math.sqrt(HEAD_DIM)
+    pix_dev = pixels // count
+    frames = frame_rows * count
+    block = frame_rows * pix_dev
+    pick = prompt_pick[0]
+    memory = text_bank[0]
+    memory = jnp.where(lax.axis_index("seq") == pick, memory, jnp.zeros_like(memory))
+    tokens = frames_in.astype(jnp.float32)
+    normed = (layer_norm(tokens) * (1.0 + modulation[1]) + modulation[0]).astype(jnp.bfloat16)
+    blocks = normed.reshape(frame_rows, count, pix_dev, width).transpose(1, 0, 2, 3)
+    blocks = blocks.reshape(count, block, width)
+    pack = jnp.concatenate(
+        [
+            self_proj.T,
+            cross_query.T,
+            cross_keyval.T,
+            jnp.concatenate([self_out.T, cross_out.T], axis=1),
+        ],
+        axis=0,
+    )
+    ends = [0]
+    for part in (self_proj, cross_query, cross_keyval, self_out):
+        ends.append(ends[-1] + part.shape[1])
+    switched, weights, text_rows = gather(blocks, pack, memory)
+
+    def full(index):
+        return weights[:, ends[index] : ends[index + 1]].reshape(-1, width)
+
+    proj, query_weight, text_weight, outs = full(0), full(1), full(2), full(3)
+    qkv = nt(switched.reshape(-1, width), proj).astype(jnp.bfloat16)
+    qkv = qkv.reshape(frames, pix_dev, 3 * attn)
+    own_keyval = nt(text_rows, text_weight).astype(jnp.bfloat16)
+    attended = temporal_attention(qkv, heads, attn, scale_q)
+    returned, keyval = give_back(attended.reshape(count, block, attn), own_keyval)
+    returned = returned.reshape(count, frame_rows, pix_dev, attn).transpose(1, 0, 2, 3)
+    self_term = nt(returned.reshape(-1, attn), outs[:, :attn])
+    after_self = (tokens.reshape(-1, width) + modulation[2] * self_term).astype(jnp.bfloat16)
+    text_len = count * text_rows.shape[0]
+    keyval = keyval.reshape(LEVELS, CORES, -1, 2 * attn).transpose(1, 0, 2, 3)
+    keyval = keyval.reshape(text_len, 2 * attn)
+    text_key = head_norm(keyval[:, :attn].astype(jnp.float32), heads).astype(jnp.bfloat16)
+    text_value = keyval[:, attn:].reshape(text_len, heads, HEAD_DIM)
+    slots = jnp.arange(text_lengths.shape[0], dtype=jnp.int32)
+    length = jnp.sum(jnp.where(slots == pick, text_lengths, 0))
+    live = jnp.arange(text_len, dtype=jnp.int32) < length
+    text_query = nt(after_self, query_weight)
+    text_query = (head_norm(text_query, heads) * scale_q).astype(jnp.bfloat16)
+    cross_scores = jnp.einsum(
+        "thd,lhd->thl", text_query, text_key, preferred_element_type=jnp.float32
+    )
+    cross_weights = jnp.where(live, jnp.exp(cross_scores), 0.0)
+    cross_total = jnp.sum(cross_weights, axis=-1)
+    cross_probs = cross_weights.astype(jnp.bfloat16)
+    cross_mix = jnp.einsum(
+        "thl,lhd->thd", cross_probs, text_value, preferred_element_type=jnp.float32
+    )
+    crossed = (cross_mix / cross_total[..., None]).astype(jnp.bfloat16).reshape(-1, attn)
+    cross_term = nt(crossed, outs[:, attn:])
+    frames_out = (after_self.astype(jnp.float32) + cross_term).astype(jnp.bfloat16)
+    return frames_out.reshape(frame_rows, pixels, width)
+
+
 def solution(mesh):
+    shared = mesh.shape["clip"] == CLIPS and mesh.shape["seq"] == LEVELS * CORES
     placed = (
         P(("clip", "seq"), None, None),
         P("clip", None),
@@ -124,7 +427,7 @@
         P(),
     )
     return jax.shard_map(
-        per_device,
+        per_device_shared if shared else per_device,
         mesh=mesh,
         in_specs=placed,
         out_specs=P(("clip", "seq"), None, None),

time: 214 us -> 153 us (0.71)
  waiting for transfers between devices: 142 us -> 0 us
  Pallas kernels: 0 us -> 110 us
  blocking collectives: 20.5 us -> 0 us
  between operations: 14.1 us -> 1.1 us
  local copies, waits for them, and re-layouts: 4.81 us -> 15.5 us
  starting transfers between devices: 10.4 us -> 0 us
  other arithmetic: 7.05 us -> 12.1 us
    pallas_call x0 -> x2, Pallas kernels: none -> 110 us  [the longest x1 73.1 us: gather(): pl.pallas_call(gather_kernel, out_shape=(jax.ShapeDtypeStruct(blocks.shap...]
    all_gather x4 -> x0, waiting for transfers between devices: 72.6 us -> none  [the longest x1 26.9 us: per_device(): lax.all_gather(self_proj, 'seq', axis=1, tiled=True)]
    psum x1 -> x0, waiting for transfers between devices: 49.6 us -> none  [spread_2(): return lax.psum(block, axis)]
    all_gather x1 -> x0, blocking collectives: 20.5 us -> none  [per_device(): keyval = lax.all_gather(own_columns, 'seq', axis=1, tiled=True)]
    all_to_all x2 -> x0, waiting for transfers between devices: 17.5 us -> none  [the longest x1 17.5 us: per_device(): lax.all_to_all(attended, 'seq', split_axis=0, concat_axis=1, tiled=True)]
    all_to_all x2 -> x0, starting transfers between devices: 10.2 us -> none  [the longest x1 6.49 us: per_device(): lax.all_to_all(normed, 'seq', split_axis=1, concat_axis=0, tiled=True)]
    slice x1 -> x4, local copies, waits for them, and re-layouts: 0.04 us -> 7.3 us  [the longest x2 5.48 us: full(): return weights[:, ends[index]:ends[index + 1]].reshape(-1, width)]
    unnamed x5 -> x0, waiting for transfers between devices: 2.48 us -> none
  transfers between devices with their start and end apart: 7 -> 0, of which waited for: 6 -> 0; matrix products, arithmetic and copies ran while one was open for 11% -> 0% of each run, Pallas kernels for 0% -> 0%
where the time goes in v1:
time: 153 us; the launch traced here: 152 us
  Pallas kernels  110 us (72%)
  local copies, waits for them, and re-layouts  15.5 us (10%)
  matrix products  13.2 us (9%)
  other arithmetic  12.1 us (8%)
    pallas_call x1, Pallas kernels, gather(): pl.pallas_call(gather_kernel, out_shape=(jax.ShapeDtypeStruct(blocks.shap...  73.1 us
    pallas_call x1, Pallas kernels, give_back(): pl.pallas_call(return_kernel, out_shape=(jax.ShapeDtypeStruct(blocks.shap...  37.3 us
    dot_general x5, matrix products, nt(): lax.dot_general(left, right, (((1,), (1,)), ((), ())), preferred_element_...  9.43 us
    slice x2, local copies, waits for them, and re-layouts, full(): return weights[:, ends[index]:ends[index + 1]].reshape(-1, width)  5.48 us

profile of v1, /device:TPU:1, one launch (start us, length us, event | category | flops | bytes accessed | tf_op | source)
XLA Modules:
  0.0 152.4 jit_solution(12401848991156063138)
XLA Ops:
  0.0 0.0 copy-start.8
  0.0 0.0 copy-start.7
  0.0 0.0 copy-start.3
  0.8 1.4 fusion.27
  2.2 1.3 iota_compare_fusion
  3.5 1.2 convert_reduce_fusion
  4.7 1.4 multiply_reduce_fusion
  6.1 0.9 slice_reduce_fusion.1
  7.0 2.2 %copy_bitcast_fusion.blocks_ref = bf16[8,32,1152]{2,1,0:T(8,128)(2,1)} fusion(bf16[4,64,1152]{2,1,0:T(8,128)(2,1)} %param.10, f32[1152]{0:T(1024)S(1)} %get-tuple-element.16, f32[1152]{0:T(1024)S(1)} %get-tuple-element.17, f32[4,64]{1,0:T(4,128)S(1)} %add_rsqrt_fusion.4, f32[4,64]{1,0:T(4,128)S(1)} %broadcast_multiply_fusion), kind=kLoop, calls=%fused_computation.38 | loop fusion | flops 1769472 | bytes 1190912 | tf_op jit(solution)/shard_map/reshape | solution.py:363
  9.1 0.9 select_bitcast_fusion.memory_ref
  10.0 0.0 copy-done.6
  10.0 0.0 copy-done.3
  10.0 1.2 fusion.6.pack_ref
  11.3 73.1 %shard_map.100 = (bf16[8,32,1152]{2,1,0:T(8,128)(2,1)}, bf16[8,576,1152]{2,1,0:T(8,128)(2,1)}, bf16[32,1152]{1,0:T(8,128)(2,1)}) custom-call(bf16[8,32,1152]{2,1,0:T(8,128)(2,1)} %copy_bitcast_fusion.blocks_ref, bf16[576,1152]{1,0:T(8,128)(2,1)} %fusion.6.pack_ref, bf16[256,1152]{1,0:T(8,128)(2,1)} %select_bitcast_fusion.memory_ref), custom_call_target="tpu_custom_call" | custom-call | tf_op jit(solution)/shard_map/pallas_call | solution.py:247
  84.4 2.5 %slice.45 = bf16[8,216,1152]{2,1,0:T(8,128)(2,1)S(1)} slice(bf16[8,576,1152]{2,1,0:T(8,128)(2,1)} %get-tuple-element.11), slice={[0:8], [0:216], [0:1152]} | slice | bytes 7962624 | tf_op jit(solution)/shard_map/slice | solution.py:379
  86.9 1.4 convolution_convert_fusion
  88.2 0.8 copy.40
  89.0 0.2 slice_convert_fusion.1
  89.2 0.5 reshape.150
  89.7 0.3 multiply_reduce_fusion.2
  90.1 0.6 reshape.133
  90.7 0.5 reshape.152
  91.2 0.3 multiply_reduce_fusion.1
  91.6 0.7 multiply_convert_fusion
  92.3 0.9 fusion.32
  93.2 0.7 fusion.9
  93.9 0.2 copy.45
  94.1 1.1 reshape_reshape.3.blocks_ref
  95.2 3.0 %fusion.30 = (bf16[8,144,1152]{2,1,0:T(8,128)(2,1)S(1)}, bf16[8,144,1152]{2,1,0:T(8,128)(2,1)S(1)}) fusion(bf16[8,576,1152]{2,1,0:T(8,128)(2,1)} %get-tuple-element.11), kind=kLoop, calls=%fused_computation.66 | loop fusion | bytes 10616832 | tf_op jit(solution)/shard_map/slice | solution.py:379
  98.2 0.0 copy-done.9
  98.2 1.5 %convolution_convert_fusion.1.text_ref = bf16[32,1152]{1,0:T(8,128)(2,1)} fusion(bf16[32,1152]{1,0:T(8,128)(2,1)S(1)} %copy-done.9, bf16[1152,1152]{1,0:T(8,128)(2,1)S(1)} %bitcast.69), kind=kOutput, calls=%fused_computation.6 | convolution fusion | flops 84971520 | bytes 2801664 | tf_op jit(solution)/shard_map/dot_general | solution.py:332
  99.7 37.3 %shard_map.101 = (bf16[8,32,576]{2,1,0:T(8,128)(2,1)}, bf16[8,32,1152]{2,1,0:T(8,128)(2,1)}) custom-call(bf16[8,32,576]{2,1,0:T(8,128)(2,1)} %reshape_reshape.3.blocks_ref, bf16[32,1152]{1,0:T(8,128)(2,1)} %convolution_convert_fusion.1.text_ref), custom_call_target="tpu_custom_call" | custom-call | tf_op jit(solution)/shard_map/pallas_call | solution.py:318
  137.1 0.0 copy-start
  137.1 1.8 %copy.46 = bf16[8,4,8,576]{3,2,0,1:T(8,128)(2,1)} copy(bf16[8,4,8,576]{3,2,1,0:T(8,128)(2,1)} %bitcast.82) | data formatting | bytes 589824 | tf_op jit(solution)/shard_map/reshape | solution.py:387
  138.9 1.1 copy.47
  140.0 0.9 fusion.31
  140.9 1.1 copy.53
  142.1 0.1 fusion.14
  142.2 1.6 %fusion.2 = bf16[256,1152]{1,0:T(8,128)(2,1)S(1)} fusion(bf16[256,576]{1,0:T(8,128)(2,1)} %bitcast.81, bf16[1152,1152]{1,0:T(8,128)(2,1)S(1)} %bitcast.75, f32[1152]{0:T(1024)S(1)} %get-tuple-element.15, bf16[256,1152]{1,0:T(8,128)(2,1)S(1)} %bitcast.70), kind=kOutput, calls=%fused_computation.5 | convolution fusion | flops 340918272 | bytes 2957312 | tf_op jit(solution)/shard_map/dot_general | solution.py:332
  143.8 0.0 copy-start.12
  143.8 0.0 copy-start.1
  143.8 0.0 copy-start.10
  143.8 3.0 %multiply_reduce_fusion.3 = (f32[256,8]{0,1:T(8,128)S(1)}, f32[256,8,72]{0,2,1:T(8,128)}) fusion(bf16[8,576,1152]{2,1,0:T(8,128)(2,1)} %get-tuple-element.11, bf16[256,1152]{1,0:T(8,128)(2,1)S(1)} %fusion.2), kind=kOutput, calls=%fused_computation.40 | convolution fusion | flops 340031488 | bytes 2514944 | tf_op jit(solution)/shard_map/dot_general | solution.py:332
  146.8 0.9 copy.48
  147.7 1.7 %bitcast_reduce_fusion = (f32[256,8]{0,1:T(8,128)S(1)}, f32[8,256,256]{2,1,0:T(8,128)S(1)}) fusion(pred[256]{0:T(512)(128)(4,1)S(1)} %copy-done.10, f32[256,8,72]{0,2,1:T(8,128)} %get-tuple-element.28, f32[256,8]{0,1:T(8,128)S(1)} %add_rsqrt_fusion.2, bf16[256,8,72]{0,2,1:T(8,128)(2,1)S(1)} %bitcast.74, f32[256,8]{0,1:T(8,128)S(1)} %add_rsqrt_fusion.3), kind=kOutput, calls=%fused_computation.7 | convolution fusion | flops 77428736 | bytes 3006720 | tf_op jit(solution)/shard_map/thd,lhd->thl/dot_general | solution.py:400
  149.4 0.5 fusion.11
  149.9 0.6 copy-done.13
  150.5 1.9 %fusion.1 = bf16[256,1152]{1,0:T(8,128)(2,1)} fusion(bf16[256,576]{0,1:T(8,128)(2,1)S(1)} %bitcast.88, bf16[1152,1152]{1,0:T(8,128)(2,1)S(1)} %bitcast.76, bf16[256,1152]{1,0:T(8,128)(2,1)S(1)} %copy-done.13), kind=kOutput, calls=%fused_computation.3 | convolution fusion | flops 340623360 | bytes 2949120 | tf_op jit(solution)/shard_map/dot_general | solution.py:332
  (23 shorter events, 0.1 us)
Async XLA Ops:
  0.0 9.1 %copy-start.2 = (bf16[1,256,1152]{2,1,0:T(8,128)(2,1)S(1)}, bf16[1,256,1152]{2,1,0:T(8,128)(2,1)}, u32[]{:S(2)}) copy-start(bf16[1,256,1152]{2,1,0:T(8,128)(2,1)} %param.17) | copy-start | bytes 1769476
  0.0 10.0 %copy-start.6 = (bf16[576,144]{0,1:T(8,128)(2,1)S(1)}, bf16[576,144]{0,1:T(8,128)(2,1)}, u32[]{:S(2)}) copy-start(bf16[576,144]{0,1:T(8,128)(2,1)} %param.16) | copy-start | bytes 497668
  0.0 10.0 %copy-start.4 = (bf16[1152,144]{0,1:T(8,128)(2,1)S(1)}, bf16[1152,144]{0,1:T(8,128)(2,1)}, u32[]{:S(2)}) copy-start(bf16[1152,144]{0,1:T(8,128)(2,1)} %param.15) | copy-start | bytes 995332
  0.0 10.0 %copy-start.8 = (bf16[1152,72]{0,1:T(8,128)(2,1)S(1)}, bf16[1152,72]{0,1:T(8,128)(2,1)}, u32[]{:S(2)}) copy-start(bf16[1152,72]{0,1:T(8,128)(2,1)} %param.14) | copy-start | bytes 497668
  0.0 10.0 %copy-start.7 = (bf16[576,144]{0,1:T(8,128)(2,1)S(1)}, bf16[576,144]{0,1:T(8,128)(2,1)}, u32[]{:S(2)}) copy-start(bf16[576,144]{0,1:T(8,128)(2,1)} %param.13) | copy-start | bytes 497668
  0.0 10.0 %copy-start.3 = (bf16[1152,216]{0,1:T(8,128)(2,1)S(1)}, bf16[1152,216]{0,1:T(8,128)(2,1)}, u32[]{:S(2)}) copy-start(bf16[1152,216]{0,1:T(8,128)(2,1)} %param.12) | copy-start | bytes 1492996
  84.4 2.5 %copy-start.11 = (bf16[8,32,1152]{2,1,0:T(8,128)(2,1)S(1)}, bf16[8,32,1152]{2,1,0:T(8,128)(2,1)}, u32[]{:S(2)}) copy-start(bf16[8,32,1152]{2,1,0:T(8,128)(2,1)} %get-tuple-element.10) | copy-start | bytes 1769476
  95.2 3.0 %copy-start.9 = (bf16[32,1152]{1,0:T(8,128)(2,1)S(1)}, bf16[32,1152]{1,0:T(8,128)(2,1)}, u32[]{:S(2)}) copy-start(bf16[32,1152]{1,0:T(8,128)(2,1)} %get-tuple-element.12) | copy-start | bytes 221188
  137.1 5.1 %copy-start = (bf16[4,64,1152]{2,1,0:T(8,128)(2,1)S(1)}, bf16[4,64,1152]{2,1,0:T(8,128)(2,1)}, u32[]{:S(2)}) copy-start(bf16[4,64,1152]{2,1,0:T(8,128)(2,1)} %param.10) | copy-start | bytes 1769476
  143.8 3.0 %copy-start.12 = (bf16[256,1152]{1,0:T(8,128)(2,1)}, bf16[256,1152]{1,0:T(8,128)(2,1)S(1)}, u32[]{:S(2)}) copy-start(bf16[256,1152]{1,0:T(8,128)(2,1)S(1)} %fusion.2) | copy-start | bytes 1769476
  143.8 3.0 %copy-start.1 = (bf16[256,576]{1,0:T(8,128)(2,1)S(1)}, bf16[256,576]{1,0:T(8,128)(2,1)}, u32[]{:S(2)}) copy-start(bf16[256,576]{1,0:T(8,128)(2,1)} %get-tuple-element.24) | copy-start | bytes 884740
  143.8 3.9 %copy-start.10 = (pred[256]{0:T(512)(128)(4,1)S(1)}, pred[256]{0:T(512)(128)(4,1)}, u32[]{:S(2)}) copy-start(pred[256]{0:T(512)(128)(4,1)} %iota_compare_fusion) | copy-start | bytes 772
  147.7 1.7 %copy-start.5 = (bf16[256,576]{0,1:T(8,128)(2,1)S(1)}, bf16[256,576]{0,1:T(8,128)(2,1)}, u32[]{:S(2)}) copy-start(bf16[256,576]{0,1:T(8,128)(2,1)} %copy.48) | copy-start | bytes 884740
  149.4 1.1 copy-start.13

commit v2 on v1

--- a/solution.py
+++ b/solution.py
@@ -144,130 +144,182 @@
     )
 
 
+SUBS = ((0, 64), (64, 48))
+OUT_ROWS, QUERY_ROWS, PROJ_ROWS = 144, 80, 224
+PACKED = OUT_ROWS + QUERY_ROWS + PROJ_ROWS
+GRANT = 56 * 1024 * 1024
+
+
 def gather_kernel(
-    blocks_ref, pack_ref, memory_ref, tokens_ref, weights_ref, rows_ref,
-    half_ref, slots_ref, held_ref,
-    block_send, block_recv, pack_send, pack_recv, local_sem, half_sem, slice_send, slice_recv,
+    frames_ref, modulation_ref, pack_ref, memory_ref, mask_ref,
+    tokens_ref, weights_ref, text_ref,
+    normed_ref, blocks_ref, masked_ref, half_ref, held_ref, slots_ref, own_ref,
+    block_send, block_recv, pack_send, pack_recv, local_sem, half_sem,
+    slice_send, slice_recv, text_send, text_recv,
 ):
     clip, seq, level, core, sibling, levels, clips = places()
     peers = [lax.rem(seq + step, LEVELS * CORES) for step in range(1, LEVELS * CORES)]
     greet([(clip, peer) for peer in peers] + [(other, seq) for other in clips])
     piece = pack_ref.shape[0] // CLIPS
     pieces = [clip] + clips
-
-    def rows(index):
-        return pl.ds(pl.multiple_of(index * piece, 16), piece)
-
-    own_rows = [pltpu.make_async_copy(pack_ref, weights_ref.at[seq], local_sem.at[0]),
-                pltpu.make_async_copy(blocks_ref.at[seq], tokens_ref.at[seq], local_sem.at[1])]
-    for copy in own_rows:
+    sends = []
+
+    def rows(part, sub):
+        start, size = SUBS[sub]
+        return pl.ds(pl.multiple_of(part * piece + start, 16), size)
+
+    def start(copy):
         copy.start()
+        sends.append(copy)
+
+    def weight(src, shard, part, sub, index, to_clip, to_seq):
+        start(remote(
+            src.at[rows(part, sub)], weights_ref.at[shard, rows(part, sub)],
+            pack_send.at[sub, index], pack_recv.at[sub, shard, part], to_clip, to_seq,
+        ))
+
+    def arrived(shard, part, sub):
+        view = weights_ref.at[shard, rows(part, sub)]
+        pltpu.make_async_copy(view, view, pack_recv.at[sub, shard, part]).wait()
+
+    for sub in range(2):
+        for n, other in enumerate(levels):
+            weight(pack_ref, seq, clip, sub, n, clip, other * CORES + core)
+    local = [pltpu.make_async_copy(pack_ref, weights_ref.at[seq], local_sem.at[0])]
+    local[0].start()
+
+    masked_ref[...] = memory_ref[...] * mask_ref[...]
     half = held_ref.shape[0]
     swap = remote(
-        memory_ref.at[pl.ds(pl.multiple_of((1 - core) * half, 16), half)], half_ref,
+        masked_ref.at[pl.ds(pl.multiple_of((1 - core) * half, 16), half)], half_ref,
         half_sem.at[0], half_sem.at[1], clip, sibling,
     )
-    swap.start()
-    sends = [swap]
-
-    def weight(src, shard, part, index, to_clip, to_seq):
-        copy = remote(
-            src, weights_ref.at[shard, rows(part)], pack_send.at[index],
-            pack_recv.at[shard, part], to_clip, to_seq,
-        )
-        copy.start()
-        sends.append(copy)
-
-    def arrived(shard, part):
-        view = weights_ref.at[shard, rows(part)]
-        pltpu.make_async_copy(view, view, pack_recv.at[shard, part]).wait()
-
+    start(swap)
+    for sub in range(2):
+        for n, part in enumerate(pieces):
+            weight(pack_ref, seq, part, sub, 3 + n, clip, sibling)
+
+    frame_rows, pixels, width = frames_ref.shape
+    gain, shift = 1.0 + modulation_ref[1:2], modulation_ref[0:1]
+    for frame in range(frame_rows):
+        normed_ref[frame] = layer_norm(frames_ref[frame].astype(jnp.float32)) * gain + shift
+    count = blocks_ref.shape[0]
+    pix = pixels // count
+    for to in range(count):
+        block = normed_ref[:, to * pix : (to + 1) * pix].reshape(frame_rows * pix, width)
+        blocks_ref[to] = block.astype(jnp.bfloat16)
+    local.append(pltpu.make_async_copy(blocks_ref.at[seq], tokens_ref.at[seq], local_sem.at[1]))
+    local[1].start()
+    for n, peer in enumerate(peers):
+        start(remote(
+            blocks_ref.at[peer], tokens_ref.at[seq], block_send.at[n], block_recv.at[seq], clip, peer
+        ))
+
+    swap.wait_recv()
+    held_ref[...] = masked_ref[pl.ds(pl.multiple_of(core * half, 16), half)] + half_ref[...]
+    size = half // LEVELS
     for n, other in enumerate(levels):
-        weight(pack_ref.at[rows(clip)], seq, clip, n, clip, other * CORES + core)
-    for n, peer in enumerate(peers):
-        copy = remote(
-            blocks_ref.at[peer], tokens_ref.at[seq], block_send.at[n], block_recv.at[seq], clip, peer
-        )
-        copy.start()
-        sends.append(copy)
-    for n, part in enumerate(pieces):
-        weight(pack_ref.at[rows(part)], seq, part, 3 + n, clip, sibling)
-
-    swap.wait_recv()
-    held_ref[...] = memory_ref[pl.ds(pl.multiple_of(core * half, 16), half)] + half_ref[...]
-    size = half // LEVELS
-    slices = []
-    for n, other in enumerate(levels):
-        copy = remote(
+        start(remote(
             held_ref.at[pl.ds(pl.multiple_of(other * size, 16), size)], slots_ref.at[level],
             slice_send.at[n], slice_recv.at[level], clip, other * CORES + core,
-        )
-        copy.start()
-        sends.append(copy)
-
-    index = 7
-    for other in levels:
-        shard = other * CORES + core
-        arrived(shard, clip)
-        for to in clips:
-            weight(weights_ref.at[shard, rows(clip)], shard, clip, index, to, seq)
+        ))
+
+    def forward(sub):
+        index = 7
+        for other in levels:
+            shard = other * CORES + core
+            arrived(shard, clip, sub)
+            for to in clips:
+                weight(weights_ref.at[shard], shard, clip, sub, index, to, seq)
+                index += 1
+            weight(weights_ref.at[shard], shard, clip, sub, index, clip, sibling)
             index += 1
-        weight(weights_ref.at[shard, rows(clip)], shard, clip, index, clip, sibling)
-        index += 1
-    for other in levels:
-        shard = other * CORES + core
-        for part in clips:
-            arrived(shard, part)
-            weight(weights_ref.at[shard, rows(part)], shard, part, index, clip, sibling)
-            index += 1
-
+
+    def across(sub):
+        index = 19
+        for other in levels:
+            shard = other * CORES + core
+            for part in clips:
+                arrived(shard, part, sub)
+                weight(weights_ref.at[shard], shard, part, sub, index, clip, sibling)
+                index += 1
+
+    def text(src, place, index, to):
+        start(remote(src, text_ref.at[place], text_send.at[index], text_recv.at[place], clip, to))
+
+    def wait(ref, sem, place):
+        pltpu.make_async_copy(ref.at[place], ref.at[place], sem.at[place]).wait()
+
+    forward(0)
     total = held_ref[pl.ds(pl.multiple_of(level * size, 16), size)]
     for other in levels:
-        pltpu.make_async_copy(slots_ref.at[other], slots_ref.at[other], slice_recv.at[other]).wait()
+        wait(slots_ref, slice_recv, other)
         total = total + slots_ref[other]
-    rows_ref[...] = total
+    own_ref[...] = total
+    place = core * LEVELS + level
+    local.append(pltpu.make_async_copy(own_ref, text_ref.at[place], local_sem.at[2]))
+    local[2].start()
+    for n, other in enumerate(levels):
+        text(own_ref, place, n, other * CORES + core)
+    text(own_ref, place, 3, sibling)
+    forward(1)
+    for n, other in enumerate(levels):
+        wait(text_ref, text_recv, core * LEVELS + other)
+        text(text_ref.at[core * LEVELS + other], core * LEVELS + other, 4 + n, sibling)
+    for sub in range(2):
+        across(sub)
     for other in [level] + levels:
         for part in pieces:
-            arrived(other * CORES + 1 - core, part)
+            for sub in range(2):
+                arrived(other * CORES + 1 - core, part, sub)
+        wait(text_ref, text_recv, (1 - core) * LEVELS + other)
     for peer in peers:
-        view = tokens_ref.at[peer]
-        pltpu.make_async_copy(view, view, block_recv.at[peer]).wait()
-    for copy in own_rows:
+        wait(tokens_ref, block_recv, peer)
+    for copy in local:
         copy.wait()
     for copy in sends:
         copy.wait_send()
 
 
-def gather(blocks, pack, memory):
-    count, rows, width = blocks.shape
-    text, dma = memory.shape[0], pltpu.SemaphoreType.DMA
+def gather(frames_in, modulation, pack, memory, mask):
+    frame_rows, pixels, width = frames_in.shape
+    count, kind, text = LEVELS * CORES, frames_in.dtype, memory.shape[0]
+    dma = pltpu.SemaphoreType.DMA
     anywhere = pl.BlockSpec(memory_space=pl.ANY)
     vmem = pl.BlockSpec(memory_space=pltpu.VMEM)
-    size = text // count
+    block, size = frame_rows * pixels // count, text // count
     return pl.pallas_call(
         gather_kernel,
         out_shape=(
-            jax.ShapeDtypeStruct(blocks.shape, blocks.dtype),
-            jax.ShapeDtypeStruct((count,) + pack.shape, pack.dtype),
-            jax.ShapeDtypeStruct((size, width), memory.dtype),
+            jax.ShapeDtypeStruct((count, block, width), kind),
+            jax.ShapeDtypeStruct((count,) + pack.shape, kind),
+            jax.ShapeDtypeStruct((count, size, width), kind),
         ),
-        in_specs=[anywhere, anywhere, vmem],
-        out_specs=(anywhere, anywhere, vmem),
+        in_specs=[vmem, vmem, anywhere, vmem, vmem],
+        out_specs=(anywhere,) * 3,
         scratch_shapes=[
-            pltpu.VMEM((text // CORES, width), memory.dtype),
-            pltpu.VMEM((LEVELS, size, width), memory.dtype),
-            pltpu.VMEM((text // CORES, width), memory.dtype),
+            pltpu.VMEM((frame_rows, pixels, width), jnp.float32),
+            pltpu.VMEM((count, block, width), kind),
+            pltpu.VMEM((text, width), kind),
+            pltpu.VMEM((text // CORES, width), kind),
+            pltpu.VMEM((text // CORES, width), kind),
+            pltpu.VMEM((LEVELS, size, width), kind),
+            pltpu.VMEM((size, width), kind),
             dma((count - 1,)),
             dma((count,)),
-            dma((28,)),
-            dma((count, CLIPS)),
-            dma((2,)),
+            dma((2, 28)),
+            dma((2, count, CLIPS)),
+            dma((3,)),
             dma((2,)),
             dma((LEVELS - 1,)),
             dma((LEVELS,)),
+            dma((7,)),
+            dma((count,)),
         ],
-        compiler_params=pltpu.CompilerParams(collective_id=0, has_side_effects=True),
-    )(blocks, pack, memory)
+        compiler_params=pltpu.CompilerParams(
+            collective_id=0, has_side_effects=True, vmem_limit_bytes=GRANT
+        ),
+    )(frames_in, modulation, pack, memory, mask)
 
 
 def return_kernel(blocks_ref, text_ref, tokens_ref, keyval_ref,
@@ -334,6 +386,84 @@
     )
 
 
+def unit(values, axis):
+    power = jnp.sum(values * values, axis=axis, keepdims=True) * (1.0 / HEAD_DIM)
+    return values * lax.rsqrt(power + EPS)
+
+
+def self_kernel(pix, tokens_ref, weights_ref, text_ref, keyval_ref, out_ref, text_out_ref, qkv_ref):
+    tokens = tokens_ref[...]
+    count = weights_ref.shape[0]
+    per = 3
+    heads = count * per // 3
+    for shard in range(count):
+        columns = nt(tokens, weights_ref[shard, OUT_ROWS + QUERY_ROWS :])
+        for j in range(per):
+            part = columns[:, j * HEAD_DIM : (j + 1) * HEAD_DIM]
+            qkv_ref[shard * per + j] = part.astype(jnp.bfloat16)
+    text_out_ref[...] = nt(keyval_ref[...], text_ref[...]).astype(jnp.bfloat16)
+    rows = tokens.shape[0]
+    row = lax.broadcasted_iota(jnp.int32, (rows, rows), 0)
+    column = lax.broadcasted_iota(jnp.int32, (rows, rows), 1)
+    same = (row % pix) == (column % pix)
+    scale_q = 1.0 / math.sqrt(HEAD_DIM)
+    outs = []
+    for head in range(heads):
+        query = (unit(qkv_ref[head].astype(jnp.float32), 1) * scale_q).astype(jnp.bfloat16)
+        key = unit(qkv_ref[heads + head].astype(jnp.float32), 1).astype(jnp.bfloat16)
+        weights = jnp.where(same, jnp.exp(nt(query, key)), 0.0)
+        total = jnp.sum(weights, axis=1, keepdims=True)
+        mixed = jnp.dot(
+            weights.astype(jnp.bfloat16), qkv_ref[2 * heads + head],
+            preferred_element_type=jnp.float32,
+        )
+        outs.append(mixed / total)
+    pad = out_ref.shape[1] - heads * HEAD_DIM
+    outs.append(jnp.zeros((rows, pad), jnp.float32))
+    out_ref[...] = jnp.concatenate(outs, axis=1).astype(jnp.bfloat16)
+
+
+def cross_kernel(
+    returned_ref, frames_ref, modulation_ref, weights_ref, keyval_ref, live_ref, out_ref,
+    attended_ref, out_weight_ref,
+):
+    count, block, lanes = returned_ref.shape
+    frame_rows, pixels, width = frames_ref.shape
+    pix = block // frame_rows
+    for src in range(count):
+        part = returned_ref[src].astype(jnp.float32)
+        for frame in range(frame_rows):
+            at = frame * pixels + src * pix
+            attended_ref[at : at + pix] = part[frame * pix : (frame + 1) * pix]
+        out_weight_ref[src * OUT_ROWS : (src + 1) * OUT_ROWS] = weights_ref[src, :OUT_ROWS]
+    self_term = nt(attended_ref[...].astype(jnp.bfloat16), out_weight_ref[:, :lanes])
+    tokens = frames_ref[...].astype(jnp.float32).reshape(frame_rows * pixels, width)
+    after_self = (tokens + modulation_ref[2:3] * self_term).astype(jnp.bfloat16)
+    live = live_ref[...] > 0.0
+    heads = count
+    scale_q = 1.0 / math.sqrt(HEAD_DIM)
+    outs = [jnp.zeros((tokens.shape[0], lanes - heads * HEAD_DIM), jnp.float32)]
+    per = keyval_ref.shape[1] // HEAD_DIM
+
+    def of_head(index):
+        shard = keyval_ref[index // per].astype(jnp.float32)
+        return shard[(index % per) * HEAD_DIM : (index % per + 1) * HEAD_DIM]
+
+    for head in range(heads):
+        query = nt(after_self, weights_ref[head, OUT_ROWS : OUT_ROWS + QUERY_ROWS])
+        query = (unit(query, 1) * scale_q).astype(jnp.bfloat16)[:, :HEAD_DIM]
+        key = unit(of_head(head), 0).astype(jnp.bfloat16)
+        scores = jnp.dot(query, key, preferred_element_type=jnp.float32)
+        weights = jnp.where(live, jnp.exp(scores), 0.0)
+        total = jnp.sum(weights, axis=1, keepdims=True)
+        value = of_head(heads + head).astype(jnp.bfloat16)
+        outs.append(nt(weights.astype(jnp.bfloat16), value) / total)
+    crossed = jnp.concatenate(outs, axis=1).astype(jnp.bfloat16)
+    cross_term = nt(crossed, out_weight_ref[:, width - lanes :])
+    result = (after_self.astype(jnp.float32) + cross_term).astype(jnp.bfloat16)
+    out_ref[...] = result.reshape(frame_rows, pixels, width)
+
+
 def per_device_shared(
     frames_in,
     modulation,
@@ -349,67 +479,48 @@
     count = lax.axis_size("seq")
     frame_rows, pixels, width = frames_in.shape
     attn = self_out.shape[0]
-    heads = attn // HEAD_DIM
-    scale_q = 1.0 / math.sqrt(HEAD_DIM)
-    pix_dev = pixels // count
-    frames = frame_rows * count
-    block = frame_rows * pix_dev
+    block = frame_rows * pixels // count
+    lanes = -(-attn // 128) * 128
     pick = prompt_pick[0]
     memory = text_bank[0]
-    memory = jnp.where(lax.axis_index("seq") == pick, memory, jnp.zeros_like(memory))
-    tokens = frames_in.astype(jnp.float32)
-    normed = (layer_norm(tokens) * (1.0 + modulation[1]) + modulation[0]).astype(jnp.bfloat16)
-    blocks = normed.reshape(frame_rows, count, pix_dev, width).transpose(1, 0, 2, 3)
-    blocks = blocks.reshape(count, block, width)
+    text_len = memory.shape[0]
+    mine = (lax.axis_index("seq") == pick).astype(jnp.bfloat16)
+    mask = jnp.full((1, width), mine)
+
+    def fill(part, rows):
+        return jnp.pad(part, ((0, rows - part.shape[0]), (0, 0)))
+
     pack = jnp.concatenate(
         [
-            self_proj.T,
-            cross_query.T,
-            cross_keyval.T,
             jnp.concatenate([self_out.T, cross_out.T], axis=1),
+            fill(cross_query.T, QUERY_ROWS),
+            fill(self_proj.T, PROJ_ROWS),
         ],
         axis=0,
     )
-    ends = [0]
-    for part in (self_proj, cross_query, cross_keyval, self_out):
-        ends.append(ends[-1] + part.shape[1])
-    switched, weights, text_rows = gather(blocks, pack, memory)
-
-    def full(index):
-        return weights[:, ends[index] : ends[index + 1]].reshape(-1, width)
-
-    proj, query_weight, text_weight, outs = full(0), full(1), full(2), full(3)
-    qkv = nt(switched.reshape(-1, width), proj).astype(jnp.bfloat16)
-    qkv = qkv.reshape(frames, pix_dev, 3 * attn)
-    own_keyval = nt(text_rows, text_weight).astype(jnp.bfloat16)
-    attended = temporal_attention(qkv, heads, attn, scale_q)
-    returned, keyval = give_back(attended.reshape(count, block, attn), own_keyval)
-    returned = returned.reshape(count, frame_rows, pix_dev, attn).transpose(1, 0, 2, 3)
-    self_term = nt(returned.reshape(-1, attn), outs[:, :attn])
-    after_self = (tokens.reshape(-1, width) + modulation[2] * self_term).astype(jnp.bfloat16)
-    text_len = count * text_rows.shape[0]
-    keyval = keyval.reshape(LEVELS, CORES, -1, 2 * attn).transpose(1, 0, 2, 3)
-    keyval = keyval.reshape(text_len, 2 * attn)
-    text_key = head_norm(keyval[:, :attn].astype(jnp.float32), heads).astype(jnp.bfloat16)
-    text_value = keyval[:, attn:].reshape(text_len, heads, HEAD_DIM)
+    switched, weights, text = gather(frames_in, modulation, pack, memory, mask)
+    attended, own_keyval = pl.pallas_call(
+        functools.partial(self_kernel, pixels // count),
+        out_shape=(
+            jax.ShapeDtypeStruct((count * block, lanes), jnp.bfloat16),
+            jax.ShapeDtypeStruct((cross_keyval.shape[1], text_len), jnp.bfloat16),
+        ),
+        scratch_shapes=[pltpu.VMEM((3 * attn // HEAD_DIM, count * block, HEAD_DIM), jnp.bfloat16)],
+        compiler_params=pltpu.CompilerParams(vmem_limit_bytes=GRANT),
+    )(switched.reshape(-1, width), weights, text.reshape(text_len, width), cross_keyval.T)
+    returned, keyval = give_back(attended.reshape(count, block, lanes), own_keyval)
     slots = jnp.arange(text_lengths.shape[0], dtype=jnp.int32)
     length = jnp.sum(jnp.where(slots == pick, text_lengths, 0))
-    live = jnp.arange(text_len, dtype=jnp.int32) < length
-    text_query = nt(after_self, query_weight)
-    text_query = (head_norm(text_query, heads) * scale_q).astype(jnp.bfloat16)
-    cross_scores = jnp.einsum(
-        "thd,lhd->thl", text_query, text_key, preferred_element_type=jnp.float32
-    )
-    cross_weights = jnp.where(live, jnp.exp(cross_scores), 0.0)
-    cross_total = jnp.sum(cross_weights, axis=-1)
-    cross_probs = cross_weights.astype(jnp.bfloat16)
-    cross_mix = jnp.einsum(
-        "thl,lhd->thd", cross_probs, text_value, preferred_element_type=jnp.float32
-    )
-    crossed = (cross_mix / cross_total[..., None]).astype(jnp.bfloat16).reshape(-1, attn)
-    cross_term = nt(crossed, outs[:, attn:])
-    frames_out = (after_self.astype(jnp.float32) + cross_term).astype(jnp.bfloat16)
-    return frames_out.reshape(frame_rows, pixels, width)
+    live = (jnp.arange(text_len, dtype=jnp.int32) < length).astype(jnp.float32)[None]
+    return pl.pallas_call(
+        cross_kernel,
+        out_shape=jax.ShapeDtypeStruct(frames_in.shape, jnp.bfloat16),
+        scratch_shapes=[
+            pltpu.VMEM((frame_rows * pixels, lanes), jnp.float32),
+            pltpu.VMEM((count * OUT_ROWS, width), jnp.bfloat16),
+        ],
+        compiler_params=pltpu.CompilerParams(vmem_limit_bytes=GRANT),
+    )(returned, frames_in, modulation, weights, keyval, live)
 
 
 def solution(mesh):

time: 153 us -> 111 us (0.73)
  local copies, waits for them, and re-layouts: 15.5 us -> 0.6 us
  matrix products: 13.2 us -> 0 us
  other arithmetic: 12.1 us -> 4.24 us
  Pallas kernels: 110 us -> 105 us
    pallas_call x1, Pallas kernels: 37.3 us -> 17.7 us  [give_back(): pl.pallas_call(return_kernel, out_shape=(jax.ShapeDtypeStruct(blocks.shap...]
    pallas_call x1 -> x3, Pallas kernels: 73.1 us -> 87 us  [the longest x1 67.5 us: gather(): pl.pallas_call(gather_kernel, out_shape=(jax.ShapeDtypeStruct((count, blo...]
    dot_general x9 -> x0, matrix products: 13.2 us -> none  [the longest x5 9.43 us: nt(): lax.dot_general(left, right, (((1,), (1,)), ((), ())), preferred_element_...]
    slice x4 -> x0, local copies, waits for them, and re-layouts: 7.3 us -> none  [the longest x2 5.48 us: full(): return weights[:, ends[index]:ends[index + 1]].reshape(-1, width)]
    reshape x5 -> x0, local copies, waits for them, and re-layouts: 4.4 us -> none  [the longest x1 1.78 us: per_device_shared(): returned.reshape(count, frame_rows, pix_dev, attn).transpose(1, 0, 2, 3)]
    reduce_sum x5 -> x0, other arithmetic: 3.35 us -> none  [the longest x1 1.37 us: layer_norm(): spread = jnp.mean(centred * centred, axis=-1, keepdims=True)]
    reshape x2 -> x0, other arithmetic: 2.36 us -> none  [the longest x1 2.17 us: per_device_shared(): blocks = blocks.reshape(count, block, width)]
    unnamed x29 -> x2, local copies, waits for them, and re-layouts: 1.76 us -> 0.01 us
where the time goes in v2:
time: 111 us; the launch traced here: 110 us
  Pallas kernels  105 us (95%)
  other arithmetic  4.24 us (4%)
    pallas_call x1, Pallas kernels, gather(): pl.pallas_call(gather_kernel, out_shape=(jax.ShapeDtypeStruct((count, blo...  67.5 us
    pallas_call x1, Pallas kernels, give_back(): pl.pallas_call(return_kernel, out_shape=(jax.ShapeDtypeStruct(blocks.shap...  17.7 us
    pallas_call x1, Pallas kernels, per_device_shared(): pl.pallas_call(cross_kernel, out_shape=jax.ShapeDtypeStruct(frames_in.sha...  10.8 us
    pallas_call x1, Pallas kernels, per_device_shared(): pl.pallas_call(functools.partial(self_kernel, pixels // count), out_shape...  8.61 us
    concatenate x1, other arithmetic, per_device_shared(): jnp.concatenate([jnp.concatenate([self_out.T, cross_out.T], axis=1), fill...  2.38 us

profile of v2, /device:TPU:1, one launch (start us, length us, event | category | flops | bytes accessed | tf_op | source)
XLA Modules:
  0.0 110.2 jit_solution(4019230346308070634)
XLA Ops:
  0.7 0.6 broadcast_in_dim.8.mask_ref
  1.3 2.4 %fusion.4.pack_ref = bf16[448,1152]{1,0:T(8,128)(2,1)} fusion(bf16[216,1152]{1,0:T(8,128)(2,1)} %bitcast.15, bf16[72,1152]{1,0:T(8,128)(2,1)} %bitcast.20, bf16[144,576]{1,0:T(8,128)(2,1)} %bitcast.18, bf16[144,576]{1,0:T(8,128)(2,1)} %bitcast.19), kind=kLoop, calls=%fused_computation.7 | loop fusion | flops 7225344 | bytes 2027520 | tf_op jit(solution)/shard_map/concatenate | solution.py:493
  3.6 67.5 %shard_map.100 = (bf16[8,32,1152]{2,1,0:T(8,128)(2,1)}, bf16[8,448,1152]{2,1,0:T(8,128)(2,1)}, bf16[8,32,1152]{2,1,0:T(8,128)(2,1)}) custom-call(bf16[4,64,1152]{2,1,0:T(8,128)(2,1)} %frames_ref.3, f32[3,1152]{1,0:T(4,128)} %modulation_ref.3, bf16[448,1152]{1,0:T(8,128)(2,1)} %fusion.4.pack_ref, bf16[256,1152]{1,0:T(8,128)(2,1)} %bitcast.14, ...), custom_call_target="tpu_custom_call" | custom-call | tf_op jit(solution)/shard_map/pallas_call | solution.py:291
  71.2 0.0 copy-start
  71.2 8.6 %shard_map.101 = (bf16[256,640]{1,0:T(8,128)(2,1)}, bf16[144,256]{1,0:T(8,128)(2,1)}) custom-call(bf16[256,1152]{1,0:T(8,128)(2,1)} %bitcast.12, bf16[8,448,1152]{2,1,0:T(8,128)(2,1)} %get-tuple-element.13.weights_ref, bf16[256,1152]{1,0:T(8,128)(2,1)} %bitcast.13, bf16[144,1152]{1,0:T(8,128)(2,1)} %bitcast.16), custom_call_target="tpu_custom_call" | custom-call | tf_op jit(solution)/shard_map/pallas_call | solution.py:502
  79.8 17.7 %shard_map.102 = (bf16[8,32,640]{2,1,0:T(8,128)(2,1)}, bf16[8,144,256]{2,1,0:T(8,128)(2,1)}) custom-call(bf16[8,32,640]{2,1,0:T(8,128)(2,1)} %bitcast.17, bf16[144,256]{1,0:T(8,128)(2,1)} %get-tuple-element.16.text_ref), custom_call_target="tpu_custom_call" | custom-call | tf_op jit(solution)/shard_map/pallas_call | solution.py:370
  97.5 0.0 copy-done
  97.5 0.6 fusion.5
  98.2 1.2 %compare_convert_fusion.live_ref = f32[1,256]{1,0:T(1,128)} fusion(s32[]{:T(128)} %fusion.5), kind=kLoop, calls=%fused_computation.9 | loop fusion | flops 512 | bytes 1028 | tf_op jit(solution)/shard_map/convert_element_type | solution.py:514
  99.4 10.8 %shard_map.103 = bf16[4,64,1152]{2,1,0:T(8,128)(2,1)} custom-call(bf16[8,32,640]{2,1,0:T(8,128)(2,1)} %get-tuple-element.17.returned_ref, bf16[4,64,1152]{2,1,0:T(8,128)(2,1)} %frames_ref.3, f32[3,1152]{1,0:T(4,128)} %modulation_ref.3, bf16[8,448,1152]{2,1,0:T(8,128)(2,1)} %get-tuple-element.13.weights_ref, ...), custom_call_target="tpu_custom_call" | custom-call | tf_op jit(solution)/shard_map/pallas_call | solution.py:515
Async XLA Ops:
  71.2 26.3 %copy-start = (s32[8]{0:T(128)S(1)}, s32[8]{0:T(128)}, u32[]{:S(2)}) copy-start(s32[8]{0:T(128)} %param.19) | copy-start | bytes 100

commit v3 on v2

--- a/solution.py
+++ b/solution.py
@@ -157,11 +157,12 @@
     block_send, block_recv, pack_send, pack_recv, local_sem, half_sem,
     slice_send, slice_recv, text_send, text_recv,
 ):
-    clip, seq, level, core, sibling, levels, clips = places()
+    clip, seq, level, core, sibling, levels, _ = places()
     peers = [lax.rem(seq + step, LEVELS * CORES) for step in range(1, LEVELS * CORES)]
-    greet([(clip, peer) for peer in peers] + [(other, seq) for other in clips])
+    beside, across, diagonal = clip + 1 - 2 * (clip % 2), (clip + 2) % 4, 3 - clip
+    greet([(clip, peer) for peer in peers] + [(beside, seq), (across, seq)])
     piece = pack_ref.shape[0] // CLIPS
-    pieces = [clip] + clips
+    pieces = [clip, beside, across, diagonal]
     sends = []
 
     def rows(part, sub):
@@ -172,19 +173,66 @@
         copy.start()
         sends.append(copy)
 
-    def weight(src, shard, part, sub, index, to_clip, to_seq):
-        start(remote(
+    def weight(src, shard, part, sub, kind, other, to_clip, to_seq):
+        return remote(
             src.at[rows(part, sub)], weights_ref.at[shard, rows(part, sub)],
-            pack_send.at[sub, index], pack_recv.at[sub, shard, part], to_clip, to_seq,
-        ))
+            pack_send.at[sub, kind, other], pack_recv.at[sub, shard, part], to_clip, to_seq,
+        )
 
     def arrived(shard, part, sub):
         view = weights_ref.at[shard, rows(part, sub)]
         pltpu.make_async_copy(view, view, pack_recv.at[sub, shard, part]).wait()
 
+    def up(sub, source):
+        return weight(
+            pack_ref if source is None else weights_ref.at[source * CORES + core],
+            seq if source is None else source * CORES + core, clip, sub, 0,
+            level if source is None else source, clip, jnp.minimum(seq + CORES, LEVELS * CORES - 1),
+        )
+
+    def down(sub, source):
+        return weight(
+            pack_ref if source is None else weights_ref.at[source * CORES + core],
+            seq if source is None else source * CORES + core, clip, sub, 1,
+            level if source is None else source, clip, jnp.maximum(seq - CORES, 0),
+        )
+
+    def climb(sub, source, act):
+        upward = level < LEVELS - 1
+        downward = level > 0
+        if source is not None:
+            upward = jnp.logical_and(upward, source < level)
+            downward = jnp.logical_and(downward, source > level)
+
+        @pl.when(upward)
+        def _():
+            act(up(sub, source))
+
+        @pl.when(downward)
+        def _():
+            act(down(sub, source))
+
+    def spread(sub, source):
+        shard = source * CORES + core
+        src = weights_ref.at[shard]
+        return [
+            weight(src, shard, clip, sub, 2, source, beside, seq),
+            weight(src, shard, clip, sub, 3, source, across, seq),
+            weight(src, shard, clip, sub, 4, source, clip, sibling),
+        ]
+
+    def turn(sub, source):
+        shard = source * CORES + core
+        part, to = (across, beside) if sub == 0 else (beside, across)
+        arrived(shard, part, sub)
+        start(weight(weights_ref.at[shard], shard, part, sub, 5, source, to, seq))
+
+    def pass_on(sub, source, part, kind):
+        shard = source * CORES + core
+        start(weight(weights_ref.at[shard], shard, part, sub, kind, source, clip, sibling))
+
     for sub in range(2):
-        for n, other in enumerate(levels):
-            weight(pack_ref, seq, clip, sub, n, clip, other * CORES + core)
+        climb(sub, None, lambda copy: copy.start())
     local = [pltpu.make_async_copy(pack_ref, weights_ref.at[seq], local_sem.at[0])]
     local[0].start()
 
@@ -197,7 +245,20 @@
     start(swap)
     for sub in range(2):
         for n, part in enumerate(pieces):
-            weight(pack_ref, seq, part, sub, 3 + n, clip, sibling)
+            start(weight(pack_ref, seq, part, sub, 2 + n, level, clip, sibling))
+
+    def step(sub, distance):
+        for source, there in (
+            (level - distance, level >= distance),
+            (level + distance, level + distance < LEVELS),
+        ):
+
+            @pl.when(there)
+            def _(source=source):
+                arrived(source * CORES + core, clip, sub)
+                climb(sub, source, lambda copy: copy.start())
+                for copy in spread(sub, source):
+                    copy.start()
 
     frame_rows, pixels, width = frames_ref.shape
     gain, shift = 1.0 + modulation_ref[1:2], modulation_ref[0:1]
@@ -208,6 +269,7 @@
     for to in range(count):
         block = normed_ref[:, to * pix : (to + 1) * pix].reshape(frame_rows * pix, width)
         blocks_ref[to] = block.astype(jnp.bfloat16)
+    step(0, 1)
     local.append(pltpu.make_async_copy(blocks_ref.at[seq], tokens_ref.at[seq], local_sem.at[1]))
     local[1].start()
     for n, peer in enumerate(peers):
@@ -224,33 +286,14 @@
             slice_send.at[n], slice_recv.at[level], clip, other * CORES + core,
         ))
 
-    def forward(sub):
-        index = 7
-        for other in levels:
-            shard = other * CORES + core
-            arrived(shard, clip, sub)
-            for to in clips:
-                weight(weights_ref.at[shard], shard, clip, sub, index, to, seq)
-                index += 1
-            weight(weights_ref.at[shard], shard, clip, sub, index, clip, sibling)
-            index += 1
-
-    def across(sub):
-        index = 19
-        for other in levels:
-            shard = other * CORES + core
-            for part in clips:
-                arrived(shard, part, sub)
-                weight(weights_ref.at[shard], shard, part, sub, index, clip, sibling)
-                index += 1
-
     def text(src, place, index, to):
         start(remote(src, text_ref.at[place], text_send.at[index], text_recv.at[place], clip, to))
 
     def wait(ref, sem, place):
         pltpu.make_async_copy(ref.at[place], ref.at[place], sem.at[place]).wait()
 
-    forward(0)
+    step(1, 1)
+    step(0, 2)
     total = held_ref[pl.ds(pl.multiple_of(level * size, 16), size)]
     for other in levels:
         wait(slots_ref, slice_recv, other)
@@ -262,12 +305,25 @@
     for n, other in enumerate(levels):
         text(own_ref, place, n, other * CORES + core)
     text(own_ref, place, 3, sibling)
-    forward(1)
+    step(1, 2)
+    step(0, 3)
+    step(1, 3)
+    for sub in range(2):
+        for source in levels:
+            turn(sub, source)
     for n, other in enumerate(levels):
         wait(text_ref, text_recv, core * LEVELS + other)
         text(text_ref.at[core * LEVELS + other], core * LEVELS + other, 4 + n, sibling)
     for sub in range(2):
-        across(sub)
+        turned, plain = (across, beside) if sub == 0 else (beside, across)
+        for source in levels:
+            pass_on(sub, source, turned, 6)
+            arrived(source * CORES + core, plain, sub)
+            pass_on(sub, source, plain, 7)
+    for sub in range(2):
+        for source in levels:
+            arrived(source * CORES + core, diagonal, sub)
+            pass_on(sub, source, diagonal, 8)
     for other in [level] + levels:
         for part in pieces:
             for sub in range(2):
@@ -277,6 +333,12 @@
         wait(tokens_ref, block_recv, peer)
     for copy in local:
         copy.wait()
+    for sub in range(2):
+        climb(sub, None, lambda copy: copy.wait_send())
+        for source in levels:
+            climb(sub, source, lambda copy: copy.wait_send())
+            for copy in spread(sub, source):
+                copy.wait_send()
     for copy in sends:
         copy.wait_send()
 
@@ -307,7 +369,7 @@
             pltpu.VMEM((size, width), kind),
             dma((count - 1,)),
             dma((count,)),
-            dma((2, 28)),
+            dma((2, 9, LEVELS)),
             dma((2, count, CLIPS)),
             dma((3,)),
             dma((2,)),
@@ -424,7 +486,7 @@
 
 
 def cross_kernel(
-    returned_ref, frames_ref, modulation_ref, weights_ref, keyval_ref, live_ref, out_ref,
+    returned_ref, frames_ref, modulation_ref, weights_ref, keyval_ref, pick_ref, lengths_ref, out_ref,
     attended_ref, out_weight_ref,
 ):
     count, block, lanes = returned_ref.shape
@@ -439,7 +501,8 @@
     self_term = nt(attended_ref[...].astype(jnp.bfloat16), out_weight_ref[:, :lanes])
     tokens = frames_ref[...].astype(jnp.float32).reshape(frame_rows * pixels, width)
     after_self = (tokens + modulation_ref[2:3] * self_term).astype(jnp.bfloat16)
-    live = live_ref[...] > 0.0
+    text_len = keyval_ref.shape[2]
+    live = lax.broadcasted_iota(jnp.int32, (1, text_len), 1) < lengths_ref[pick_ref[0]]
     heads = count
     scale_q = 1.0 / math.sqrt(HEAD_DIM)
     outs = [jnp.zeros((tokens.shape[0], lanes - heads * HEAD_DIM), jnp.float32)]
@@ -509,18 +572,17 @@
         compiler_params=pltpu.CompilerParams(vmem_limit_bytes=GRANT),
     )(switched.reshape(-1, width), weights, text.reshape(text_len, width), cross_keyval.T)
     returned, keyval = give_back(attended.reshape(count, block, lanes), own_keyval)
-    slots = jnp.arange(text_lengths.shape[0], dtype=jnp.int32)
-    length = jnp.sum(jnp.where(slots == pick, text_lengths, 0))
-    live = (jnp.arange(text_len, dtype=jnp.int32) < length).astype(jnp.float32)[None]
     return pl.pallas_call(
         cross_kernel,
         out_shape=jax.ShapeDtypeStruct(frames_in.shape, jnp.bfloat16),
+        in_specs=[pl.BlockSpec(memory_space=pltpu.VMEM)] * 5
+        + [pl.BlockSpec(memory_space=pltpu.SMEM)] * 2,
         scratch_shapes=[
             pltpu.VMEM((frame_rows * pixels, lanes), jnp.float32),
             pltpu.VMEM((count * OUT_ROWS, width), jnp.bfloat16),
         ],
         compiler_params=pltpu.CompilerParams(vmem_limit_bytes=GRANT),
-    )(returned, frames_in, modulation, weights, keyval, live)
+    )(returned, frames_in, modulation, weights, keyval, prompt_pick, text_lengths)
 
 
 def solution(mesh):

time: 111 us -> 101 us (0.910)
  Pallas kernels: 105 us -> 97.6 us
  other arithmetic: 4.24 us -> 2.37 us
    pallas_call x1, Pallas kernels: 67.5 us -> 62 us  [gather(): pl.pallas_call(gather_kernel, out_shape=(jax.ShapeDtypeStruct((count, blo...]
    pallas_call x1, Pallas kernels: 17.7 us -> 16.1 us  [give_back(): pl.pallas_call(return_kernel, out_shape=(jax.ShapeDtypeStruct(blocks.shap...]
    convert_element_type x1 -> x0, other arithmetic: 1.24 us -> none  [per_device_shared(): (jnp.arange(text_len, dtype=jnp.int32) < length).astype(jnp.float32)[None]]
where the time goes in v3:
time: 101 us
  Pallas kernels  97.6 us (97%)
  other arithmetic  2.37 us (2%)
    pallas_call x1, Pallas kernels, gather(): pl.pallas_call(gather_kernel, out_shape=(jax.ShapeDtypeStruct((count, blo...  62 us
    pallas_call x1, Pallas kernels, give_back(): pl.pallas_call(return_kernel, out_shape=(jax.ShapeDtypeStruct(blocks.shap...  16.1 us
    pallas_call x1, Pallas kernels, per_device_shared(): pl.pallas_call(cross_kernel, out_shape=jax.ShapeDtypeStruct(frames_in.sha...  10.8 us
    pallas_call x1, Pallas kernels, per_device_shared(): pl.pallas_call(functools.partial(self_kernel, pixels // count), out_shape...  8.62 us
    concatenate x1, other arithmetic, per_device_shared(): jnp.concatenate([jnp.concatenate([self_out.T, cross_out.T], axis=1), fill...  2.37 us

profile of v3, /device:TPU:1, one launch (start us, length us, event | category | flops | bytes accessed | tf_op | source)
XLA Modules:
  0.0 101.2 jit_solution(3926629272125327559)
XLA Ops:
  0.7 0.6 broadcast_in_dim.3.mask_ref
  1.3 2.4 %fusion.4.pack_ref = bf16[448,1152]{1,0:T(8,128)(2,1)} fusion(bf16[216,1152]{1,0:T(8,128)(2,1)} %bitcast.14, bf16[72,1152]{1,0:T(8,128)(2,1)} %bitcast.19, bf16[144,576]{1,0:T(8,128)(2,1)} %bitcast.17, bf16[144,576]{1,0:T(8,128)(2,1)} %bitcast.18), kind=kLoop, calls=%fused_computation.7 | loop fusion | flops 7225344 | bytes 2027520 | tf_op jit(solution)/shard_map/concatenate | solution.py:556
  3.6 62.0 %shard_map.100 = (bf16[8,32,1152]{2,1,0:T(8,128)(2,1)}, bf16[8,448,1152]{2,1,0:T(8,128)(2,1)}, bf16[8,32,1152]{2,1,0:T(8,128)(2,1)}) custom-call(bf16[4,64,1152]{2,1,0:T(8,128)(2,1)} %frames_ref.3, f32[3,1152]{1,0:T(4,128)} %modulation_ref.3, bf16[448,1152]{1,0:T(8,128)(2,1)} %fusion.4.pack_ref, bf16[256,1152]{1,0:T(8,128)(2,1)} %bitcast.13, ...), custom_call_target="tpu_custom_call" | custom-call | tf_op jit(solution)/shard_map/pallas_call | solution.py:353
  65.6 8.6 %shard_map.101 = (bf16[256,640]{1,0:T(8,128)(2,1)}, bf16[144,256]{1,0:T(8,128)(2,1)}) custom-call(bf16[256,1152]{1,0:T(8,128)(2,1)} %bitcast.11, bf16[8,448,1152]{2,1,0:T(8,128)(2,1)} %get-tuple-element.13.weights_ref, bf16[256,1152]{1,0:T(8,128)(2,1)} %bitcast.12, bf16[144,1152]{1,0:T(8,128)(2,1)} %bitcast.15), custom_call_target="tpu_custom_call" | custom-call | tf_op jit(solution)/shard_map/pallas_call | solution.py:565
  74.3 16.1 %shard_map.102 = (bf16[8,32,640]{2,1,0:T(8,128)(2,1)}, bf16[8,144,256]{2,1,0:T(8,128)(2,1)}) custom-call(bf16[8,32,640]{2,1,0:T(8,128)(2,1)} %bitcast.16, bf16[144,256]{1,0:T(8,128)(2,1)} %get-tuple-element.16.text_ref), custom_call_target="tpu_custom_call" | custom-call | tf_op jit(solution)/shard_map/pallas_call | solution.py:432
  90.4 10.8 %shard_map.103 = bf16[4,64,1152]{2,1,0:T(8,128)(2,1)} custom-call(bf16[8,32,640]{2,1,0:T(8,128)(2,1)} %get-tuple-element.17.returned_ref, bf16[4,64,1152]{2,1,0:T(8,128)(2,1)} %frames_ref.3, f32[3,1152]{1,0:T(4,128)} %modulation_ref.3, bf16[8,448,1152]{2,1,0:T(8,128)(2,1)} %get-tuple-element.13.weights_ref, ...), custom_call_target="tpu_custom_call" | custom-call | tf_op jit(solution)/shard_map/pallas_call | solution.py:575

commit v4 on v3

--- a/solution.py
+++ b/solution.py
@@ -1,4 +1,3 @@
-import functools
 import math
 
 import jax
@@ -145,29 +144,112 @@
 
 
 SUBS = ((0, 64), (64, 48))
-OUT_ROWS, QUERY_ROWS, PROJ_ROWS = 144, 80, 224
-PACKED = OUT_ROWS + QUERY_ROWS + PROJ_ROWS
+PROJ_ROWS, OUT_ROWS, QUERY_ROWS = 224, 144, 80
 GRANT = 56 * 1024 * 1024
 
 
-def gather_kernel(
-    frames_ref, modulation_ref, pack_ref, memory_ref, mask_ref,
-    tokens_ref, weights_ref, text_ref,
+def nt(left, right):
+    return lax.dot_general(
+        left, right, (((1,), (1,)), ((), ())), preferred_element_type=jnp.float32
+    )
+
+
+def unit(values, axis):
+    power = jnp.sum(values * values, axis=axis, keepdims=True) * (1.0 / HEAD_DIM)
+    return values * lax.rsqrt(power + EPS)
+
+
+def project(tokens, weights_ref, qkv_ref):
+    per = 3
+    for shard in range(weights_ref.shape[0]):
+        columns = nt(tokens, weights_ref[shard, :PROJ_ROWS])
+        for j in range(per):
+            part = columns[:, j * HEAD_DIM : (j + 1) * HEAD_DIM]
+            qkv_ref[shard * per + j] = part.astype(jnp.bfloat16)
+
+
+def self_head(qkv_ref, head, heads, pix):
+    rows = qkv_ref.shape[1]
+    row = lax.broadcasted_iota(jnp.int32, (rows, rows), 0)
+    column = lax.broadcasted_iota(jnp.int32, (rows, rows), 1)
+    same = (row % pix) == (column % pix)
+    scale_q = 1.0 / math.sqrt(HEAD_DIM)
+    query = (unit(qkv_ref[head].astype(jnp.float32), 1) * scale_q).astype(jnp.bfloat16)
+    key = unit(qkv_ref[heads + head].astype(jnp.float32), 1).astype(jnp.bfloat16)
+    weights = jnp.where(same, jnp.exp(nt(query, key)), 0.0)
+    total = jnp.sum(weights, axis=1, keepdims=True)
+    mixed = jnp.dot(
+        weights.astype(jnp.bfloat16), qkv_ref[2 * heads + head],
+        preferred_element_type=jnp.float32,
+    )
+    return mixed / total
+
+
+def sublayers(
+    returned_ref, frames_ref, modulation_ref, weights_ref, keyval_ref, pick_ref, lengths_ref,
+    out_ref, attended_ref, out_weight_ref,
+):
+    count, block, lanes = returned_ref.shape
+    frame_rows, pixels, width = frames_ref.shape
+    pix = block // frame_rows
+    for src in range(count):
+        part = returned_ref[src].astype(jnp.float32)
+        for frame in range(frame_rows):
+            at = frame * pixels + src * pix
+            attended_ref[at : at + pix] = part[frame * pix : (frame + 1) * pix]
+        out_weight_ref[src * OUT_ROWS : (src + 1) * OUT_ROWS] = weights_ref[
+            src, PROJ_ROWS : PROJ_ROWS + OUT_ROWS
+        ]
+    self_term = nt(attended_ref[...].astype(jnp.bfloat16), out_weight_ref[:, :lanes])
+    tokens = frames_ref[...].astype(jnp.float32).reshape(frame_rows * pixels, width)
+    after_self = (tokens + modulation_ref[2:3] * self_term).astype(jnp.bfloat16)
+    text_len = keyval_ref.shape[2]
+    live = lax.broadcasted_iota(jnp.int32, (1, text_len), 1) < lengths_ref[pick_ref[0]]
+    heads = count
+    scale_q = 1.0 / math.sqrt(HEAD_DIM)
+    outs = [jnp.zeros((tokens.shape[0], lanes - heads * HEAD_DIM), jnp.float32)]
+    per = keyval_ref.shape[1] // HEAD_DIM
+
+    def of_head(index):
+        shard = keyval_ref[index // per].astype(jnp.float32)
+        return shard[(index % per) * HEAD_DIM : (index % per + 1) * HEAD_DIM]
+
+    for head in range(heads):
+        query = nt(after_self, weights_ref[head, PROJ_ROWS + OUT_ROWS :])
+        query = (unit(query, 1) * scale_q).astype(jnp.bfloat16)[:, :HEAD_DIM]
+        key = unit(of_head(head), 0).astype(jnp.bfloat16)
+        scores = jnp.dot(query, key, preferred_element_type=jnp.float32)
+        weights = jnp.where(live, jnp.exp(scores), 0.0)
+        total = jnp.sum(weights, axis=1, keepdims=True)
+        value = of_head(heads + head).astype(jnp.bfloat16)
+        outs.append(nt(weights.astype(jnp.bfloat16), value) / total)
+    crossed = jnp.concatenate(outs, axis=1).astype(jnp.bfloat16)
+    cross_term = nt(crossed, out_weight_ref[:, width - lanes :])
+    result = (after_self.astype(jnp.float32) + cross_term).astype(jnp.bfloat16)
+    out_ref[...] = result.reshape(frame_rows, pixels, width)
+
+
+def block_kernel(
+    frames_ref, modulation_ref, pack_ref, memory_ref, mask_ref, text_weight_ref,
+    pick_ref, lengths_ref,
+    out_ref,
+    tokens_ref, weights_ref, text_ref, qkv_ref, mixed_ref, returned_ref, columns_ref, keyval_ref,
+    attended_ref, out_weight_ref,
     normed_ref, blocks_ref, masked_ref, half_ref, held_ref, slots_ref, own_ref,
     block_send, block_recv, pack_send, pack_recv, local_sem, half_sem,
     slice_send, slice_recv, text_send, text_recv,
+    back_send, back_recv, keyval_send, keyval_recv,
 ):
     clip, seq, level, core, sibling, levels, _ = places()
     peers = [lax.rem(seq + step, LEVELS * CORES) for step in range(1, LEVELS * CORES)]
     beside, across, diagonal = clip + 1 - 2 * (clip % 2), (clip + 2) % 4, 3 - clip
     greet([(clip, peer) for peer in peers] + [(beside, seq), (across, seq)])
-    piece = pack_ref.shape[0] // CLIPS
     pieces = [clip, beside, across, diagonal]
     sends = []
 
     def rows(part, sub):
-        start, size = SUBS[sub]
-        return pl.ds(pl.multiple_of(part * piece + start, 16), size)
+        first, size = SUBS[sub]
+        return pl.ds(pl.multiple_of(CLIPS * first + part * size, 16), size)
 
     def start(copy):
         copy.start()
@@ -231,8 +313,7 @@
         shard = source * CORES + core
         start(weight(weights_ref.at[shard], shard, part, sub, kind, source, clip, sibling))
 
-    for sub in range(2):
-        climb(sub, None, lambda copy: copy.start())
+    climb(0, None, lambda copy: copy.start())
     local = [pltpu.make_async_copy(pack_ref, weights_ref.at[seq], local_sem.at[0])]
     local[0].start()
 
@@ -243,9 +324,12 @@
         half_sem.at[0], half_sem.at[1], clip, sibling,
     )
     start(swap)
-    for sub in range(2):
+
+    def to_sibling(sub):
         for n, part in enumerate(pieces):
             start(weight(pack_ref, seq, part, sub, 2 + n, level, clip, sibling))
+
+    to_sibling(0)
 
     def step(sub, distance):
         for source, there in (
@@ -292,7 +376,6 @@
     def wait(ref, sem, place):
         pltpu.make_async_copy(ref.at[place], ref.at[place], sem.at[place]).wait()
 
-    step(1, 1)
     step(0, 2)
     total = held_ref[pl.ds(pl.multiple_of(level * size, 16), size)]
     for other in levels:
@@ -305,34 +388,85 @@
     for n, other in enumerate(levels):
         text(own_ref, place, n, other * CORES + core)
     text(own_ref, place, 3, sibling)
-    step(1, 2)
     step(0, 3)
-    step(1, 3)
-    for sub in range(2):
+    climb(1, None, lambda copy: copy.start())
+
+    def finish(sub):
+        turned, plain = (across, beside) if sub == 0 else (beside, across)
         for source in levels:
             turn(sub, source)
-    for n, other in enumerate(levels):
-        wait(text_ref, text_recv, core * LEVELS + other)
-        text(text_ref.at[core * LEVELS + other], core * LEVELS + other, 4 + n, sibling)
-    for sub in range(2):
-        turned, plain = (across, beside) if sub == 0 else (beside, across)
         for source in levels:
             pass_on(sub, source, turned, 6)
             arrived(source * CORES + core, plain, sub)
             pass_on(sub, source, plain, 7)
-    for sub in range(2):
         for source in levels:
             arrived(source * CORES + core, diagonal, sub)
             pass_on(sub, source, diagonal, 8)
+
+    def complete(sub):
+        for other in [level] + levels:
+            for part in pieces:
+                arrived(other * CORES + 1 - core, part, sub)
+
+    finish(0)
+    to_sibling(1)
+    for n, other in enumerate(levels):
+        wait(text_ref, text_recv, core * LEVELS + other)
+        text(text_ref.at[core * LEVELS + other], core * LEVELS + other, 4 + n, sibling)
+    step(1, 1)
     for other in [level] + levels:
-        for part in pieces:
-            for sub in range(2):
-                arrived(other * CORES + 1 - core, part, sub)
         wait(text_ref, text_recv, (1 - core) * LEVELS + other)
+    local[2].wait()
+    memory = text_ref[...].reshape(count * text_ref.shape[1], width)
+    columns_ref[...] = nt(text_weight_ref[...], memory).astype(jnp.bfloat16)
+
+    def keyval(src, shard, index, to):
+        start(remote(
+            src, keyval_ref.at[shard], keyval_send.at[index], keyval_recv.at[shard], clip, to
+        ))
+
+    local.append(pltpu.make_async_copy(columns_ref, keyval_ref.at[seq], local_sem.at[3]))
+    local[3].start()
+    for n, other in enumerate(levels):
+        keyval(columns_ref, seq, n, other * CORES + core)
+    keyval(columns_ref, seq, 3, sibling)
+    complete(0)
     for peer in peers:
         wait(tokens_ref, block_recv, peer)
-    for copy in local:
-        copy.wait()
+    local[0].wait()
+    local[1].wait()
+    project(tokens_ref[...].reshape(frame_rows * pixels, width), weights_ref, qkv_ref)
+    step(1, 2)
+    heads = qkv_ref.shape[0] // 3
+    outs = [self_head(qkv_ref, head, heads, pix) for head in range(heads // 2)]
+    step(1, 3)
+    outs += [self_head(qkv_ref, head, heads, pix) for head in range(heads // 2, heads)]
+    lanes = mixed_ref.shape[2]
+    outs.append(jnp.zeros((frame_rows * pixels, lanes - heads * HEAD_DIM), jnp.float32))
+    mixed = jnp.concatenate(outs, axis=1).astype(jnp.bfloat16)
+    mixed_ref[...] = mixed.reshape(mixed_ref.shape)
+    local.append(pltpu.make_async_copy(mixed_ref.at[seq], returned_ref.at[seq], local_sem.at[4]))
+    local[4].start()
+    for n, peer in enumerate(peers):
+        start(remote(
+            mixed_ref.at[peer], returned_ref.at[seq], back_send.at[n], back_recv.at[seq], clip, peer
+        ))
+    for n, other in enumerate(levels):
+        shard = other * CORES + core
+        wait(keyval_ref, keyval_recv, shard)
+        keyval(keyval_ref.at[shard], shard, 4 + n, sibling)
+    finish(1)
+    complete(1)
+    for other in [level] + levels:
+        wait(keyval_ref, keyval_recv, other * CORES + 1 - core)
+    for peer in peers:
+        wait(returned_ref, back_recv, peer)
+    local[3].wait()
+    local[4].wait()
+    sublayers(
+        returned_ref, frames_ref, modulation_ref, weights_ref, keyval_ref, pick_ref, lengths_ref,
+        out_ref, attended_ref, out_weight_ref,
+    )
     for sub in range(2):
         climb(sub, None, lambda copy: copy.wait_send())
         for source in levels:
@@ -343,23 +477,31 @@
         copy.wait_send()
 
 
-def gather(frames_in, modulation, pack, memory, mask):
+def whole_block(frames_in, modulation, pack, memory, mask, text_weight, prompt_pick, text_lengths):
     frame_rows, pixels, width = frames_in.shape
     count, kind, text = LEVELS * CORES, frames_in.dtype, memory.shape[0]
-    dma = pltpu.SemaphoreType.DMA
-    anywhere = pl.BlockSpec(memory_space=pl.ANY)
-    vmem = pl.BlockSpec(memory_space=pltpu.VMEM)
-    block, size = frame_rows * pixels // count, text // count
+    dma, vmem = pltpu.SemaphoreType.DMA, pl.BlockSpec(memory_space=pltpu.VMEM)
+    smem = pl.BlockSpec(memory_space=pltpu.SMEM)
+    tokens = frame_rows * pixels
+    block, size, columns = tokens // count, text // count, text_weight.shape[0]
+    heads = count
+    lanes = -(-heads * HEAD_DIM // 128) * 128
     return pl.pallas_call(
-        gather_kernel,
-        out_shape=(
-            jax.ShapeDtypeStruct((count, block, width), kind),
-            jax.ShapeDtypeStruct((count,) + pack.shape, kind),
-            jax.ShapeDtypeStruct((count, size, width), kind),
-        ),
-        in_specs=[vmem, vmem, anywhere, vmem, vmem],
-        out_specs=(anywhere,) * 3,
+        block_kernel,
+        out_shape=jax.ShapeDtypeStruct(frames_in.shape, kind),
+        in_specs=[vmem, vmem, vmem, vmem, vmem, vmem, smem, smem],
+        out_specs=vmem,
         scratch_shapes=[
+            pltpu.VMEM((count, block, width), kind),
+            pltpu.VMEM((count,) + pack.shape, kind),
+            pltpu.VMEM((count, size, width), kind),
+            pltpu.VMEM((3 * heads, tokens, HEAD_DIM), kind),
+            pltpu.VMEM((count, block, lanes), kind),
+            pltpu.VMEM((count, block, lanes), kind),
+            pltpu.VMEM((columns, text), kind),
+            pltpu.VMEM((count, columns, text), kind),
+            pltpu.VMEM((tokens, lanes), jnp.float32),
+            pltpu.VMEM((count * OUT_ROWS, width), kind),
             pltpu.VMEM((frame_rows, pixels, width), jnp.float32),
             pltpu.VMEM((count, block, width), kind),
             pltpu.VMEM((text, width), kind),
@@ -371,160 +513,21 @@
             dma((count,)),
             dma((2, 9, LEVELS)),
             dma((2, count, CLIPS)),
-            dma((3,)),
+            dma((5,)),
             dma((2,)),
             dma((LEVELS - 1,)),
             dma((LEVELS,)),
+            dma((7,)),
+            dma((count,)),
+            dma((count - 1,)),
+            dma((count,)),
             dma((7,)),
             dma((count,)),
         ],
         compiler_params=pltpu.CompilerParams(
             collective_id=0, has_side_effects=True, vmem_limit_bytes=GRANT
         ),
-    )(frames_in, modulation, pack, memory, mask)
-
-
-def return_kernel(blocks_ref, text_ref, tokens_ref, keyval_ref,
-                  block_send, block_recv, text_send, text_recv, local_sem):
-    clip, seq, level, core, sibling, levels, _ = places()
-    peers = [lax.rem(seq + step, LEVELS * CORES) for step in range(1, LEVELS * CORES)]
-    greet([(clip, peer) for peer in peers])
-    own = [pltpu.make_async_copy(text_ref, keyval_ref.at[seq], local_sem.at[0]),
-           pltpu.make_async_copy(blocks_ref.at[seq], tokens_ref.at[seq], local_sem.at[1])]
-    for copy in own:
-        copy.start()
-    sends = []
-
-    def text(src, shard, index, to):
-        copy = remote(src, keyval_ref.at[shard], text_send.at[index], text_recv.at[shard], clip, to)
-        copy.start()
-        sends.append(copy)
-
-    def arrived(ref, sem, shard):
-        pltpu.make_async_copy(ref.at[shard], ref.at[shard], sem.at[shard]).wait()
-
-    for n, other in enumerate(levels):
-        text(text_ref, seq, n, other * CORES + core)
-    for n, peer in enumerate(peers):
-        copy = remote(
-            blocks_ref.at[peer], tokens_ref.at[seq], block_send.at[n], block_recv.at[seq], clip, peer
-        )
-        copy.start()
-        sends.append(copy)
-    text(text_ref, seq, 3, sibling)
-    for n, other in enumerate(levels):
-        shard = other * CORES + core
-        arrived(keyval_ref, text_recv, shard)
-        text(keyval_ref.at[shard], shard, 4 + n, sibling)
-    for other in [level] + levels:
-        arrived(keyval_ref, text_recv, other * CORES + 1 - core)
-    for peer in peers:
-        arrived(tokens_ref, block_recv, peer)
-    for copy in own:
-        copy.wait()
-    for copy in sends:
-        copy.wait_send()
-
-
-def give_back(blocks, text):
-    count, dma = blocks.shape[0], pltpu.SemaphoreType.DMA
-    anywhere = pl.BlockSpec(memory_space=pl.ANY)
-    return pl.pallas_call(
-        return_kernel,
-        out_shape=(
-            jax.ShapeDtypeStruct(blocks.shape, blocks.dtype),
-            jax.ShapeDtypeStruct((count,) + text.shape, text.dtype),
-        ),
-        in_specs=[anywhere, anywhere],
-        out_specs=(anywhere, anywhere),
-        scratch_shapes=[dma((count - 1,)), dma((count,)), dma((7,)), dma((count,)), dma((2,))],
-        compiler_params=pltpu.CompilerParams(collective_id=1, has_side_effects=True),
-    )(blocks, text)
-
-
-def nt(left, right):
-    return lax.dot_general(
-        left, right, (((1,), (1,)), ((), ())), preferred_element_type=jnp.float32
-    )
-
-
-def unit(values, axis):
-    power = jnp.sum(values * values, axis=axis, keepdims=True) * (1.0 / HEAD_DIM)
-    return values * lax.rsqrt(power + EPS)
-
-
-def self_kernel(pix, tokens_ref, weights_ref, text_ref, keyval_ref, out_ref, text_out_ref, qkv_ref):
-    tokens = tokens_ref[...]
-    count = weights_ref.shape[0]
-    per = 3
-    heads = count * per // 3
-    for shard in range(count):
-        columns = nt(tokens, weights_ref[shard, OUT_ROWS + QUERY_ROWS :])
-        for j in range(per):
-            part = columns[:, j * HEAD_DIM : (j + 1) * HEAD_DIM]
-            qkv_ref[shard * per + j] = part.astype(jnp.bfloat16)
-    text_out_ref[...] = nt(keyval_ref[...], text_ref[...]).astype(jnp.bfloat16)
-    rows = tokens.shape[0]
-    row = lax.broadcasted_iota(jnp.int32, (rows, rows), 0)
-    column = lax.broadcasted_iota(jnp.int32, (rows, rows), 1)
-    same = (row % pix) == (column % pix)
-    scale_q = 1.0 / math.sqrt(HEAD_DIM)
-    outs = []
-    for head in range(heads):
-        query = (unit(qkv_ref[head].astype(jnp.float32), 1) * scale_q).astype(jnp.bfloat16)
-        key = unit(qkv_ref[heads + head].astype(jnp.float32), 1).astype(jnp.bfloat16)
-        weights = jnp.where(same, jnp.exp(nt(query, key)), 0.0)
-        total = jnp.sum(weights, axis=1, keepdims=True)
-        mixed = jnp.dot(
-            weights.astype(jnp.bfloat16), qkv_ref[2 * heads + head],
-            preferred_element_type=jnp.float32,
-        )
-        outs.append(mixed / total)
-    pad = out_ref.shape[1] - heads * HEAD_DIM
-    outs.append(jnp.zeros((rows, pad), jnp.float32))
-    out_ref[...] = jnp.concatenate(outs, axis=1).astype(jnp.bfloat16)
-
-
-def cross_kernel(
-    returned_ref, frames_ref, modulation_ref, weights_ref, keyval_ref, pick_ref, lengths_ref, out_ref,
-    attended_ref, out_weight_ref,
-):
-    count, block, lanes = returned_ref.shape
-    frame_rows, pixels, width = frames_ref.shape
-    pix = block // frame_rows
-    for src in range(count):
-        part = returned_ref[src].astype(jnp.float32)
-        for frame in range(frame_rows):
-            at = frame * pixels + src * pix
-            attended_ref[at : at + pix] = part[frame * pix : (frame + 1) * pix]
-        out_weight_ref[src * OUT_ROWS : (src + 1) * OUT_ROWS] = weights_ref[src, :OUT_ROWS]
-    self_term = nt(attended_ref[...].astype(jnp.bfloat16), out_weight_ref[:, :lanes])
-    tokens = frames_ref[...].astype(jnp.float32).reshape(frame_rows * pixels, width)
-    after_self = (tokens + modulation_ref[2:3] * self_term).astype(jnp.bfloat16)
-    text_len = keyval_ref.shape[2]
-    live = lax.broadcasted_iota(jnp.int32, (1, text_len), 1) < lengths_ref[pick_ref[0]]
-    heads = count
-    scale_q = 1.0 / math.sqrt(HEAD_DIM)
-    outs = [jnp.zeros((tokens.shape[0], lanes - heads * HEAD_DIM), jnp.float32)]
-    per = keyval_ref.shape[1] // HEAD_DIM
-
-    def of_head(index):
-        shard = keyval_ref[index // per].astype(jnp.float32)
-        return shard[(index % per) * HEAD_DIM : (index % per + 1) * HEAD_DIM]
-
-    for head in range(heads):
-        query = nt(after_self, weights_ref[head, OUT_ROWS : OUT_ROWS + QUERY_ROWS])
-        query = (unit(query, 1) * scale_q).astype(jnp.bfloat16)[:, :HEAD_DIM]
-        key = unit(of_head(head), 0).astype(jnp.bfloat16)
-        scores = jnp.dot(query, key, preferred_element_type=jnp.float32)
-        weights = jnp.where(live, jnp.exp(scores), 0.0)
-        total = jnp.sum(weights, axis=1, keepdims=True)
-        value = of_head(heads + head).astype(jnp.bfloat16)
-        outs.append(nt(weights.astype(jnp.bfloat16), value) / total)
-    crossed = jnp.concatenate(outs, axis=1).astype(jnp.bfloat16)
-    cross_term = nt(crossed, out_weight_ref[:, width - lanes :])
-    result = (after_self.astype(jnp.float32) + cross_term).astype(jnp.bfloat16)
-    out_ref[...] = result.reshape(frame_rows, pixels, width)
+    )(frames_in, modulation, pack, memory, mask, text_weight, prompt_pick, text_lengths)
 
 
 def per_device_shared(
@@ -539,50 +542,25 @@
     prompt_pick,
     text_lengths,
 ):
-    count = lax.axis_size("seq")
-    frame_rows, pixels, width = frames_in.shape
-    attn = self_out.shape[0]
-    block = frame_rows * pixels // count
-    lanes = -(-attn // 128) * 128
     pick = prompt_pick[0]
     memory = text_bank[0]
-    text_len = memory.shape[0]
     mine = (lax.axis_index("seq") == pick).astype(jnp.bfloat16)
-    mask = jnp.full((1, width), mine)
+    mask = jnp.full((1, frames_in.shape[2]), mine)
 
     def fill(part, rows):
         return jnp.pad(part, ((0, rows - part.shape[0]), (0, 0)))
 
     pack = jnp.concatenate(
         [
+            fill(self_proj.T, PROJ_ROWS),
             jnp.concatenate([self_out.T, cross_out.T], axis=1),
             fill(cross_query.T, QUERY_ROWS),
-            fill(self_proj.T, PROJ_ROWS),
         ],
         axis=0,
     )
-    switched, weights, text = gather(frames_in, modulation, pack, memory, mask)
-    attended, own_keyval = pl.pallas_call(
-        functools.partial(self_kernel, pixels // count),
-        out_shape=(
-            jax.ShapeDtypeStruct((count * block, lanes), jnp.bfloat16),
-            jax.ShapeDtypeStruct((cross_keyval.shape[1], text_len), jnp.bfloat16),
-        ),
-        scratch_shapes=[pltpu.VMEM((3 * attn // HEAD_DIM, count * block, HEAD_DIM), jnp.bfloat16)],
-        compiler_params=pltpu.CompilerParams(vmem_limit_bytes=GRANT),
-    )(switched.reshape(-1, width), weights, text.reshape(text_len, width), cross_keyval.T)
-    returned, keyval = give_back(attended.reshape(count, block, lanes), own_keyval)
-    return pl.pallas_call(
-        cross_kernel,
-        out_shape=jax.ShapeDtypeStruct(frames_in.shape, jnp.bfloat16),
-        in_specs=[pl.BlockSpec(memory_space=pltpu.VMEM)] * 5
-        + [pl.BlockSpec(memory_space=pltpu.SMEM)] * 2,
-        scratch_shapes=[
-            pltpu.VMEM((frame_rows * pixels, lanes), jnp.float32),
-            pltpu.VMEM((count * OUT_ROWS, width), jnp.bfloat16),
-        ],
-        compiler_params=pltpu.CompilerParams(vmem_limit_bytes=GRANT),
-    )(returned, frames_in, modulation, weights, keyval, prompt_pick, text_lengths)
+    return whole_block(
+        frames_in, modulation, pack, memory, mask, cross_keyval.T, prompt_pick, text_lengths
+    )
 
 
 def solution(mesh):

time: 101 us -> 87.2 us (0.86)
  Pallas kernels: 97.6 us -> 81.4 us
  local copies, waits for them, and re-layouts: 0.6 us -> 2.52 us
    pallas_call x4 -> x1, Pallas kernels: 97.6 us -> 81.4 us  [whole_block(): pl.pallas_call(block_kernel, out_shape=jax.ShapeDtypeStruct(frames_in.sha...]
    unnamed x0 -> x1, local copies, waits for them, and re-layouts: none -> 1.92 us
where the time goes in v4:
time: 87.2 us; the launch traced here: 87 us
  Pallas kernels  81.4 us (93%)
  local copies, waits for them, and re-layouts  2.52 us (3%)
  other arithmetic  2.41 us (3%)
    pallas_call x1, Pallas kernels, whole_block(): pl.pallas_call(block_kernel, out_shape=jax.ShapeDtypeStruct(frames_in.sha...  81.4 us
    concatenate x1, other arithmetic, per_device_shared(): jnp.concatenate([fill(self_proj.T, PROJ_ROWS), jnp.concatenate([self_out....  2.41 us
    unnamed x1, local copies, waits for them, and re-layouts  1.92 us

profile of v4, /device:TPU:1, one launch (start us, length us, event | category | flops | bytes accessed | tf_op | source)
XLA Modules:
  0.0 87.0 jit_solution(9871102495649246228)
XLA Ops:
  0.7 0.6 broadcast_in_dim.3.mask_ref
  1.3 2.4 %fusion.2.pack_ref = bf16[448,1152]{1,0:T(8,128)(2,1)} fusion(bf16[72,1152]{1,0:T(8,128)(2,1)} %bitcast.13, bf16[144,576]{1,0:T(8,128)(2,1)} %bitcast.11, bf16[144,576]{1,0:T(8,128)(2,1)} %bitcast.12, bf16[216,1152]{1,0:T(8,128)(2,1)} %bitcast.9), kind=kLoop, calls=%fused_computation.4 | loop fusion | flops 6193152 | bytes 2027520 | tf_op jit(solution)/shard_map/concatenate | solution.py:553
  3.7 81.4 %shard_map.100 = bf16[4,64,1152]{2,1,0:T(8,128)(2,1)} custom-call(bf16[4,64,1152]{2,1,0:T(8,128)(2,1)} %frames_ref.1, f32[3,1152]{1,0:T(4,128)} %modulation_ref.1, bf16[448,1152]{1,0:T(8,128)(2,1)} %fusion.2.pack_ref, bf16[256,1152]{1,0:T(8,128)(2,1)} %bitcast.8, bf16[1,1152]{1,0:T(2,128)(2,1)} %broadcast_in_dim.3.mask_ref, bf16[144,1152]{1,0:T(8,128)(2,1)} %bitcast.10, ...), custom_call_target="tpu_custom_call" | custom-call | tf_op jit(solution)/shard_map/pallas_call | solution.py:489
  85.1 1.9 %copy.13 = bf16[4,64,1152]{2,1,0:T(8,128)(2,1)} copy(bf16[4,64,1152]{2,1,0:T(8,128)(2,1)} %shard_map.100) | data formatting | bytes 1179648

commit v5 on v4

--- a/solution.py
+++ b/solution.py
@@ -185,8 +185,15 @@
     return mixed / total
 
 
+def assemble(weights_ref, out_weight_ref, query_weight_ref):
+    outs = PROJ_ROWS + OUT_ROWS
+    for src in range(weights_ref.shape[0]):
+        out_weight_ref[src * OUT_ROWS : (src + 1) * OUT_ROWS] = weights_ref[src, PROJ_ROWS:outs]
+        query_weight_ref[src * QUERY_ROWS : (src + 1) * QUERY_ROWS] = weights_ref[src, outs:]
+
+
 def sublayers(
-    returned_ref, frames_ref, modulation_ref, weights_ref, keyval_ref, pick_ref, lengths_ref,
+    returned_ref, frames_ref, modulation_ref, query_weight_ref, keyval_ref, pick_ref, lengths_ref,
     out_ref, attended_ref, out_weight_ref,
 ):
     count, block, lanes = returned_ref.shape
@@ -197,9 +204,6 @@
         for frame in range(frame_rows):
             at = frame * pixels + src * pix
             attended_ref[at : at + pix] = part[frame * pix : (frame + 1) * pix]
-        out_weight_ref[src * OUT_ROWS : (src + 1) * OUT_ROWS] = weights_ref[
-            src, PROJ_ROWS : PROJ_ROWS + OUT_ROWS
-        ]
     self_term = nt(attended_ref[...].astype(jnp.bfloat16), out_weight_ref[:, :lanes])
     tokens = frames_ref[...].astype(jnp.float32).reshape(frame_rows * pixels, width)
     after_self = (tokens + modulation_ref[2:3] * self_term).astype(jnp.bfloat16)
@@ -214,9 +218,10 @@
         shard = keyval_ref[index // per].astype(jnp.float32)
         return shard[(index % per) * HEAD_DIM : (index % per + 1) * HEAD_DIM]
 
+    queries = nt(after_self, query_weight_ref[...])
     for head in range(heads):
-        query = nt(after_self, weights_ref[head, PROJ_ROWS + OUT_ROWS :])
-        query = (unit(query, 1) * scale_q).astype(jnp.bfloat16)[:, :HEAD_DIM]
+        query = queries[:, head * QUERY_ROWS : head * QUERY_ROWS + HEAD_DIM]
+        query = (unit(query, 1) * scale_q).astype(jnp.bfloat16)
         key = unit(of_head(head), 0).astype(jnp.bfloat16)
         scores = jnp.dot(query, key, preferred_element_type=jnp.float32)
         weights = jnp.where(live, jnp.exp(scores), 0.0)
@@ -234,7 +239,7 @@
     pick_ref, lengths_ref,
     out_ref,
     tokens_ref, weights_ref, text_ref, qkv_ref, mixed_ref, returned_ref, columns_ref, keyval_ref,
-    attended_ref, out_weight_ref,
+    attended_ref, out_weight_ref, query_weight_ref,
     normed_ref, blocks_ref, masked_ref, half_ref, held_ref, slots_ref, own_ref,
     block_send, block_recv, pack_send, pack_recv, local_sem, half_sem,
     slice_send, slice_recv, text_send, text_recv,
@@ -361,6 +366,15 @@
             blocks_ref.at[peer], tokens_ref.at[seq], block_send.at[n], block_recv.at[seq], clip, peer
         ))
 
+    def text(src, place, index, to):
+        start(remote(src, text_ref.at[place], text_send.at[index], text_recv.at[place], clip, to))
+
+    def wait(ref, sem, place):
+        pltpu.make_async_copy(ref.at[place], ref.at[place], sem.at[place]).wait()
+
+    step(0, 2)
+    step(0, 3)
+    climb(1, None, lambda copy: copy.start())
     swap.wait_recv()
     held_ref[...] = masked_ref[pl.ds(pl.multiple_of(core * half, 16), half)] + half_ref[...]
     size = half // LEVELS
@@ -370,13 +384,25 @@
             slice_send.at[n], slice_recv.at[level], clip, other * CORES + core,
         ))
 
-    def text(src, place, index, to):
-        start(remote(src, text_ref.at[place], text_send.at[index], text_recv.at[place], clip, to))
-
-    def wait(ref, sem, place):
-        pltpu.make_async_copy(ref.at[place], ref.at[place], sem.at[place]).wait()
-
-    step(0, 2)
+    def finish(sub):
+        turned, plain = (across, beside) if sub == 0 else (beside, across)
+        for source in levels:
+            turn(sub, source)
+        for source in levels:
+            pass_on(sub, source, turned, 6)
+            arrived(source * CORES + core, plain, sub)
+            pass_on(sub, source, plain, 7)
+        for source in levels:
+            arrived(source * CORES + core, diagonal, sub)
+            pass_on(sub, source, diagonal, 8)
+
+    def complete(sub):
+        for other in [level] + levels:
+            for part in pieces:
+                arrived(other * CORES + 1 - core, part, sub)
+
+    finish(0)
+    to_sibling(1)
     total = held_ref[pl.ds(pl.multiple_of(level * size, 16), size)]
     for other in levels:
         wait(slots_ref, slice_recv, other)
@@ -388,58 +414,36 @@
     for n, other in enumerate(levels):
         text(own_ref, place, n, other * CORES + core)
     text(own_ref, place, 3, sibling)
-    step(0, 3)
-    climb(1, None, lambda copy: copy.start())
-
-    def finish(sub):
-        turned, plain = (across, beside) if sub == 0 else (beside, across)
-        for source in levels:
-            turn(sub, source)
-        for source in levels:
-            pass_on(sub, source, turned, 6)
-            arrived(source * CORES + core, plain, sub)
-            pass_on(sub, source, plain, 7)
-        for source in levels:
-            arrived(source * CORES + core, diagonal, sub)
-            pass_on(sub, source, diagonal, 8)
-
-    def complete(sub):
-        for other in [level] + levels:
-            for part in pieces:
-                arrived(other * CORES + 1 - core, part, sub)
-
-    finish(0)
-    to_sibling(1)
-    for n, other in enumerate(levels):
-        wait(text_ref, text_recv, core * LEVELS + other)
-        text(text_ref.at[core * LEVELS + other], core * LEVELS + other, 4 + n, sibling)
     step(1, 1)
-    for other in [level] + levels:
-        wait(text_ref, text_recv, (1 - core) * LEVELS + other)
-    local[2].wait()
-    memory = text_ref[...].reshape(count * text_ref.shape[1], width)
-    columns_ref[...] = nt(text_weight_ref[...], memory).astype(jnp.bfloat16)
 
     def keyval(src, shard, index, to):
         start(remote(
             src, keyval_ref.at[shard], keyval_send.at[index], keyval_recv.at[shard], clip, to
         ))
 
-    local.append(pltpu.make_async_copy(columns_ref, keyval_ref.at[seq], local_sem.at[3]))
-    local[3].start()
-    for n, other in enumerate(levels):
-        keyval(columns_ref, seq, n, other * CORES + core)
-    keyval(columns_ref, seq, 3, sibling)
     complete(0)
     for peer in peers:
         wait(tokens_ref, block_recv, peer)
     local[0].wait()
     local[1].wait()
     project(tokens_ref[...].reshape(frame_rows * pixels, width), weights_ref, qkv_ref)
+    for n, other in enumerate(levels):
+        wait(text_ref, text_recv, core * LEVELS + other)
+        text(text_ref.at[core * LEVELS + other], core * LEVELS + other, 4 + n, sibling)
     step(1, 2)
     heads = qkv_ref.shape[0] // 3
     outs = [self_head(qkv_ref, head, heads, pix) for head in range(heads // 2)]
     step(1, 3)
+    for other in [level] + levels:
+        wait(text_ref, text_recv, (1 - core) * LEVELS + other)
+    local[2].wait()
+    memory = text_ref[...].reshape(count * text_ref.shape[1], width)
+    columns_ref[...] = nt(text_weight_ref[...], memory).astype(jnp.bfloat16)
+    local.append(pltpu.make_async_copy(columns_ref, keyval_ref.at[seq], local_sem.at[3]))
+    local[3].start()
+    for n, other in enumerate(levels):
+        keyval(columns_ref, seq, n, other * CORES + core)
+    keyval(columns_ref, seq, 3, sibling)
     outs += [self_head(qkv_ref, head, heads, pix) for head in range(heads // 2, heads)]
     lanes = mixed_ref.shape[2]
     outs.append(jnp.zeros((frame_rows * pixels, lanes - heads * HEAD_DIM), jnp.float32))
@@ -457,6 +461,7 @@
         keyval(keyval_ref.at[shard], shard, 4 + n, sibling)
     finish(1)
     complete(1)
+    assemble(weights_ref, out_weight_ref, query_weight_ref)
     for other in [level] + levels:
         wait(keyval_ref, keyval_recv, other * CORES + 1 - core)
     for peer in peers:
@@ -464,7 +469,8 @@
     local[3].wait()
     local[4].wait()
     sublayers(
-        returned_ref, frames_ref, modulation_ref, weights_ref, keyval_ref, pick_ref, lengths_ref,
+        returned_ref, frames_ref, modulation_ref, query_weight_ref, keyval_ref, pick_ref,
+        lengths_ref,
         out_ref, attended_ref, out_weight_ref,
     )
     for sub in range(2):
@@ -502,6 +508,7 @@
             pltpu.VMEM((count, columns, text), kind),
             pltpu.VMEM((tokens, lanes), jnp.float32),
             pltpu.VMEM((count * OUT_ROWS, width), kind),
+            pltpu.VMEM((count * QUERY_ROWS, width), kind),
             pltpu.VMEM((frame_rows, pixels, width), jnp.float32),
             pltpu.VMEM((count, block, width), kind),
             pltpu.VMEM((text, width), kind),

time: 87.2 us -> 87 us (level)
  the two profiles are of different devices: /device:TPU:1 before, /device:TPU:9 now
where the time goes in v5:
time: 87 us; the launch traced here: 86.8 us
  Pallas kernels  81.2 us (93%)
  local copies, waits for them, and re-layouts  2.52 us (3%)
  other arithmetic  2.41 us (3%)
    pallas_call x1, Pallas kernels, whole_block(): pl.pallas_call(block_kernel, out_shape=jax.ShapeDtypeStruct(frames_in.sha...  81.2 us
    concatenate x1, other arithmetic, per_device_shared(): jnp.concatenate([fill(self_proj.T, PROJ_ROWS), jnp.concatenate([self_out....  2.41 us
    unnamed x1, local copies, waits for them, and re-layouts  1.92 us

profile of v5, /device:TPU:9, one launch (start us, length us, event | category | flops | bytes accessed | tf_op | source)
XLA Modules:
  0.0 86.8 jit_solution(2571272671925728671)
XLA Ops:
  0.7 0.6 broadcast_in_dim.3.mask_ref
  1.3 2.4 %fusion.2.pack_ref = bf16[448,1152]{1,0:T(8,128)(2,1)} fusion(bf16[72,1152]{1,0:T(8,128)(2,1)} %bitcast.13, bf16[144,576]{1,0:T(8,128)(2,1)} %bitcast.11, bf16[144,576]{1,0:T(8,128)(2,1)} %bitcast.12, bf16[216,1152]{1,0:T(8,128)(2,1)} %bitcast.9), kind=kLoop, calls=%fused_computation.4 | loop fusion | flops 6193152 | bytes 2027520 | tf_op jit(solution)/shard_map/concatenate | solution.py:560
  3.7 81.2 %shard_map.100 = bf16[4,64,1152]{2,1,0:T(8,128)(2,1)} custom-call(bf16[4,64,1152]{2,1,0:T(8,128)(2,1)} %frames_ref.1, f32[3,1152]{1,0:T(4,128)} %modulation_ref.1, bf16[448,1152]{1,0:T(8,128)(2,1)} %fusion.2.pack_ref, bf16[256,1152]{1,0:T(8,128)(2,1)} %bitcast.8, bf16[1,1152]{1,0:T(2,128)(2,1)} %broadcast_in_dim.3.mask_ref, bf16[144,1152]{1,0:T(8,128)(2,1)} %bitcast.10, ...), custom_call_target="tpu_custom_call" | custom-call | tf_op jit(solution)/shard_map/pallas_call | solution.py:495
  84.9 1.9 %copy.13 = bf16[4,64,1152]{2,1,0:T(8,128)(2,1)} copy(bf16[4,64,1152]{2,1,0:T(8,128)(2,1)} %shard_map.100) | data formatting | bytes 1179648

commit v6 on v5

--- a/solution.py
+++ b/solution.py
@@ -384,14 +384,18 @@
             slice_send.at[n], slice_recv.at[level], clip, other * CORES + core,
         ))
 
-    def finish(sub):
-        turned, plain = (across, beside) if sub == 0 else (beside, across)
+    def turn_all(sub):
         for source in levels:
             turn(sub, source)
+
+    def beside_all(sub):
+        turned, plain = (across, beside) if sub == 0 else (beside, across)
         for source in levels:
             pass_on(sub, source, turned, 6)
             arrived(source * CORES + core, plain, sub)
             pass_on(sub, source, plain, 7)
+
+    def diagonal_all(sub):
         for source in levels:
             arrived(source * CORES + core, diagonal, sub)
             pass_on(sub, source, diagonal, 8)
@@ -401,7 +405,10 @@
             for part in pieces:
                 arrived(other * CORES + 1 - core, part, sub)
 
-    finish(0)
+    turn_all(0)
+    beside_all(0)
+    step(1, 1)
+    diagonal_all(0)
     to_sibling(1)
     total = held_ref[pl.ds(pl.multiple_of(level * size, 16), size)]
     for other in levels:
@@ -414,26 +421,26 @@
     for n, other in enumerate(levels):
         text(own_ref, place, n, other * CORES + core)
     text(own_ref, place, 3, sibling)
-    step(1, 1)
 
     def keyval(src, shard, index, to):
         start(remote(
             src, keyval_ref.at[shard], keyval_send.at[index], keyval_recv.at[shard], clip, to
         ))
 
+    step(1, 2)
     complete(0)
     for peer in peers:
         wait(tokens_ref, block_recv, peer)
     local[0].wait()
     local[1].wait()
     project(tokens_ref[...].reshape(frame_rows * pixels, width), weights_ref, qkv_ref)
+    step(1, 3)
     for n, other in enumerate(levels):
         wait(text_ref, text_recv, core * LEVELS + other)
         text(text_ref.at[core * LEVELS + other], core * LEVELS + other, 4 + n, sibling)
-    step(1, 2)
     heads = qkv_ref.shape[0] // 3
     outs = [self_head(qkv_ref, head, heads, pix) for head in range(heads // 2)]
-    step(1, 3)
+    turn_all(1)
     for other in [level] + levels:
         wait(text_ref, text_recv, (1 - core) * LEVELS + other)
     local[2].wait()
@@ -455,11 +462,12 @@
         start(remote(
             mixed_ref.at[peer], returned_ref.at[seq], back_send.at[n], back_recv.at[seq], clip, peer
         ))
+    beside_all(1)
+    diagonal_all(1)
     for n, other in enumerate(levels):
         shard = other * CORES + core
         wait(keyval_ref, keyval_recv, shard)
         keyval(keyval_ref.at[shard], shard, 4 + n, sibling)
-    finish(1)
     complete(1)
     assemble(weights_ref, out_weight_ref, query_weight_ref)
     for other in [level] + levels:

time: 87 us -> 81.7 us (0.939)
  the two profiles are of different devices: /device:TPU:9 before, /device:TPU:1 now
where the time goes in v6:
time: 81.7 us; the launch traced here: 81.5 us
  Pallas kernels  75.9 us (93%)
  local copies, waits for them, and re-layouts  2.52 us (3%)
  other arithmetic  2.41 us (3%)
    pallas_call x1, Pallas kernels, whole_block(): pl.pallas_call(block_kernel, out_shape=jax.ShapeDtypeStruct(frames_in.sha...  75.9 us
    concatenate x1, other arithmetic, per_device_shared(): jnp.concatenate([fill(self_proj.T, PROJ_ROWS), jnp.concatenate([self_out....  2.41 us
    unnamed x1, local copies, waits for them, and re-layouts  1.92 us

profile of v6, /device:TPU:1, one launch (start us, length us, event | category | flops | bytes accessed | tf_op | source)
XLA Modules:
  0.0 81.5 jit_solution(13021825763210886439)
XLA Ops:
  0.7 0.6 broadcast_in_dim.3.mask_ref
  1.3 2.4 %fusion.2.pack_ref = bf16[448,1152]{1,0:T(8,128)(2,1)} fusion(bf16[72,1152]{1,0:T(8,128)(2,1)} %bitcast.13, bf16[144,576]{1,0:T(8,128)(2,1)} %bitcast.11, bf16[144,576]{1,0:T(8,128)(2,1)} %bitcast.12, bf16[216,1152]{1,0:T(8,128)(2,1)} %bitcast.9), kind=kLoop, calls=%fused_computation.4 | loop fusion | flops 6193152 | bytes 2027520 | tf_op jit(solution)/shard_map/concatenate | solution.py:568
  3.7 75.9 %shard_map.100 = bf16[4,64,1152]{2,1,0:T(8,128)(2,1)} custom-call(bf16[4,64,1152]{2,1,0:T(8,128)(2,1)} %frames_ref.1, f32[3,1152]{1,0:T(4,128)} %modulation_ref.1, bf16[448,1152]{1,0:T(8,128)(2,1)} %fusion.2.pack_ref, bf16[256,1152]{1,0:T(8,128)(2,1)} %bitcast.8, bf16[1,1152]{1,0:T(2,128)(2,1)} %broadcast_in_dim.3.mask_ref, bf16[144,1152]{1,0:T(8,128)(2,1)} %bitcast.10, ...), custom_call_target="tpu_custom_call" | custom-call | tf_op jit(solution)/shard_map/pallas_call | solution.py:503
  79.5 1.9 %copy.13 = bf16[4,64,1152]{2,1,0:T(8,128)(2,1)} copy(bf16[4,64,1152]{2,1,0:T(8,128)(2,1)} %shard_map.100) | data formatting | bytes 1179648

commit v7 on v6

--- a/solution.py
+++ b/solution.py
@@ -429,18 +429,19 @@
 
     step(1, 2)
     complete(0)
+    step(1, 3)
     for peer in peers:
         wait(tokens_ref, block_recv, peer)
     local[0].wait()
     local[1].wait()
     project(tokens_ref[...].reshape(frame_rows * pixels, width), weights_ref, qkv_ref)
-    step(1, 3)
+    turn_all(1)
     for n, other in enumerate(levels):
         wait(text_ref, text_recv, core * LEVELS + other)
         text(text_ref.at[core * LEVELS + other], core * LEVELS + other, 4 + n, sibling)
     heads = qkv_ref.shape[0] // 3
     outs = [self_head(qkv_ref, head, heads, pix) for head in range(heads // 2)]
-    turn_all(1)
+    beside_all(1)
     for other in [level] + levels:
         wait(text_ref, text_recv, (1 - core) * LEVELS + other)
     local[2].wait()
@@ -462,7 +463,6 @@
         start(remote(
             mixed_ref.at[peer], returned_ref.at[seq], back_send.at[n], back_recv.at[seq], clip, peer
         ))
-    beside_all(1)
     diagonal_all(1)
     for n, other in enumerate(levels):
         shard = other * CORES + core

time: 81.7 us -> 81.7 us (level)
  no operation moved by 1% of the time
where the time goes in v7:
time: 81.7 us; the launch traced here: 81.5 us
  Pallas kernels  75.9 us (93%)
  local copies, waits for them, and re-layouts  2.52 us (3%)
  other arithmetic  2.41 us (3%)
    pallas_call x1, Pallas kernels, whole_block(): pl.pallas_call(block_kernel, out_shape=jax.ShapeDtypeStruct(frames_in.sha...  75.9 us
    concatenate x1, other arithmetic, per_device_shared(): jnp.concatenate([fill(self_proj.T, PROJ_ROWS), jnp.concatenate([self_out....  2.41 us
    unnamed x1, local copies, waits for them, and re-layouts  1.92 us

profile of v7, /device:TPU:1, one launch (start us, length us, event | category | flops | bytes accessed | tf_op | source)
XLA Modules:
  0.0 81.5 jit_solution(2007949744224620469)
XLA Ops:
  0.7 0.6 broadcast_in_dim.3.mask_ref
  1.3 2.4 %fusion.2.pack_ref = bf16[448,1152]{1,0:T(8,128)(2,1)} fusion(bf16[72,1152]{1,0:T(8,128)(2,1)} %bitcast.13, bf16[144,576]{1,0:T(8,128)(2,1)} %bitcast.11, bf16[144,576]{1,0:T(8,128)(2,1)} %bitcast.12, bf16[216,1152]{1,0:T(8,128)(2,1)} %bitcast.9), kind=kLoop, calls=%fused_computation.4 | loop fusion | flops 6193152 | bytes 2027520 | tf_op jit(solution)/shard_map/concatenate | solution.py:568
  3.7 75.9 %shard_map.100 = bf16[4,64,1152]{2,1,0:T(8,128)(2,1)} custom-call(bf16[4,64,1152]{2,1,0:T(8,128)(2,1)} %frames_ref.1, f32[3,1152]{1,0:T(4,128)} %modulation_ref.1, bf16[448,1152]{1,0:T(8,128)(2,1)} %fusion.2.pack_ref, bf16[256,1152]{1,0:T(8,128)(2,1)} %bitcast.8, bf16[1,1152]{1,0:T(2,128)(2,1)} %broadcast_in_dim.3.mask_ref, bf16[144,1152]{1,0:T(8,128)(2,1)} %bitcast.10, ...), custom_call_target="tpu_custom_call" | custom-call | tf_op jit(solution)/shard_map/pallas_call | solution.py:503
  79.6 1.9 %copy.13 = bf16[4,64,1152]{2,1,0:T(8,128)(2,1)} copy(bf16[4,64,1152]{2,1,0:T(8,128)(2,1)} %shard_map.100) | data formatting | bytes 1179648
